TPU v7x, 32 devices: a whole 2x2x4 slice. The times are simulated.
32 devices in a mesh: pipe: 8 (over z, x), dp: 4 (over y, core).
Axes of the slice: x: 2, y: 2, z: 4, core: 2. Of those that a mesh axis runs over, the one named last changes fastest.
Arguments:
- parked: bfloat16 [8, 8, 128, 8192], P('pipe', 'dp'), may hold values from -160 to 160
- slot_order: int32 [8, 4, 2], P('pipe', 'dp'), may hold values from 0 to 1, each once within a row
- segment_ids: int32 [8, 8, 128], P('pipe', 'dp'), may hold values from 0 to 3, never falling along the last dimension, each value on 1 to 64 neighbouring positions
- queries: bfloat16 [8, 8, 128, 4096], P('pipe', 'dp'), may hold values from -17 to 17
- out_grad: bfloat16 [8, 8, 128, 4096], P('pipe', 'dp'), may hold values from -4 to 4
- norm_gain: bfloat16 [8, 8192], P('pipe'), may hold values from 0.5 to 1.5
- kv_weight: bfloat16 [8, 8192, 1024], P('pipe', 'dp'), may hold values from -0.0625 to 0.0625
Outputs:
- upstream_grad: bfloat16 [8, 8, 128, 8192], P('pipe', 'dp')
- kv_weight_grad: bfloat16 [8, 8192, 1024], P('pipe', 'dp')
- gain_grad: float32 [8, 8192], P('pipe')
All inputs are finite; a program needn't handle non-finite values.
Results may differ from a plain program's by a relative error of at most 0.012.
The roundings to bfloat16 on the way count: a program that leaves them out, or rounds other values in their place, can miss the bound.
Values may be sent and summed in bfloat16 or wider, within the bound.
A program may use at most 128 MiB of HBM per device.

v0:
```python
import math

import jax
import jax.numpy as jnp
from jax import lax
from jax.sharding import PartitionSpec as P

QH = 32
KVH = 4
HD = 128


EPSILON = 1e-05


def shifted(value, axis, steps):
    count = lax.axis_size(axis)
    leading, last = (max(0, -steps), min(count, count - steps))
    return lax.ppermute(value, axis, [(source, source + steps) for source in range(leading, last)])


def attention_grads(queries, out_grad, keys, values, segments):
    batch_count = queries.shape[0]
    seq_len = queries.shape[1]
    group_size = QH // KVH
    scaling = 1.0 / math.sqrt(HD)
    query_heads = queries.reshape(batch_count, seq_len, KVH, group_size, HD)
    grad_heads = out_grad.reshape(batch_count, seq_len, KVH, group_size, HD)
    key_heads = keys.reshape(batch_count, seq_len, KVH, HD)
    value_heads = values.reshape(batch_count, seq_len, KVH, HD)
    scores = (
        jnp.einsum("bqhgd,bkhd->bhgqk", query_heads, key_heads, preferred_element_type=jnp.float32)
        * scaling
    )
    position = jnp.arange(seq_len)
    causal = position[None, :] <= position[:, None]
    allowed = causal[None] & (segments[:, :, None] == segments[:, None, :])
    scores = jnp.where(allowed[:, None, None], scores, -1e30)
    highest = jnp.max(scores, axis=-1, keepdims=True)
    weights = jnp.exp(scores - highest)
    probabilities = weights / jnp.sum(weights, axis=-1, keepdims=True)
    probs_low = probabilities.astype(jnp.bfloat16)
    value_grad = jnp.einsum(
        "bhgqk,bqhgd->bkhd", probs_low, grad_heads, preferred_element_type=jnp.float32
    )
    prob_grad = jnp.einsum(
        "bqhgd,bkhd->bhgqk", grad_heads, value_heads, preferred_element_type=jnp.float32
    )
    row_dot = jnp.sum(probabilities * prob_grad, axis=-1, keepdims=True)
    score_grad = (probabilities * (prob_grad - row_dot) * scaling).astype(jnp.bfloat16)
    key_grad = jnp.einsum(
        "bhgqk,bqhgd->bkhd", score_grad, query_heads, preferred_element_type=jnp.float32
    )
    key_low = key_grad.astype(jnp.bfloat16).reshape(batch_count, seq_len, KVH * HD)
    value_low = value_grad.astype(jnp.bfloat16).reshape(batch_count, seq_len, KVH * HD)
    return jnp.concatenate([key_low, value_low], axis=-1)


def local(parked, slot_order, segment_ids, queries, out_grad, norm_gain, kv_weight):
    sections = lax.axis_size("pipe")
    stored = parked[0]
    micro_count, seq_len, feature_count = stored.shape
    token_count = micro_count * seq_len
    flat_stored = stored.reshape(token_count, feature_count)
    spread = lax.all_to_all(flat_stored, "pipe", split_axis=1, concat_axis=0, tiled=True)
    blocks = spread.reshape(sections, token_count, feature_count // sections)[::-1]
    fetched = lax.all_to_all(blocks, "pipe", split_axis=0, concat_axis=2, tiled=True).reshape(
        micro_count, seq_len, feature_count
    )
    inputs = jnp.take(fetched, slot_order[0, 0], axis=0)
    flat_inputs = inputs.reshape(token_count, feature_count)
    inputs_wide = flat_inputs.astype(jnp.float32)
    inverse = lax.rsqrt(jnp.mean(inputs_wide * inputs_wide, axis=-1) + EPSILON)
    gain_full = norm_gain[0].astype(jnp.float32)
    local_weight = kv_weight[0]
    slice_width = local_weight.shape[0]
    start_col = lax.axis_index("dp") * slice_width
    gain_local = lax.dynamic_slice_in_dim(gain_full, start_col, slice_width)
    columns = lax.all_to_all(flat_inputs, "dp", split_axis=1, concat_axis=0, tiled=True)
    scales = lax.all_gather(inverse, "dp", axis=0, tiled=True)
    columns_wide = columns.astype(jnp.float32)
    normed_cols = (columns_wide * scales[:, None] * gain_local).astype(jnp.bfloat16)
    normed = (inputs_wide * inverse[:, None] * gain_full).astype(jnp.bfloat16)
    full_weight = lax.all_gather(local_weight, "dp", axis=0, tiled=True)
    projected = jnp.dot(normed, full_weight, preferred_element_type=jnp.float32)
    projected_low = projected.astype(jnp.bfloat16).reshape(micro_count, seq_len, -1)
    head_span = projected_low.shape[-1] // 2
    kv_grads = attention_grads(
        queries[0],
        out_grad[0],
        projected_low[..., :head_span],
        projected_low[..., head_span:],
        segment_ids[0],
    )
    kv_grads = kv_grads.reshape(token_count, -1)
    all_kv_grads = lax.all_gather(kv_grads, "dp", axis=0, tiled=True)
    weight_grad = lax.dot_general(
        normed_cols, all_kv_grads, (((0,), (0,)), ((), ())), preferred_element_type=jnp.float32
    ).astype(jnp.bfloat16)
    normed_grad = lax.dot_general(
        kv_grads, full_weight, (((1,), (1,)), ((), ())), preferred_element_type=jnp.float32
    )
    scaled_grad = normed_grad * gain_full
    inner_mean = jnp.mean(scaled_grad * inputs_wide, axis=-1)
    scale_col = inverse[:, None]
    input_grad = (
        scale_col * scaled_grad - inputs_wide * scale_col**3 * inner_mean[:, None]
    ).astype(jnp.bfloat16)
    gain_term = jnp.sum(normed_grad * inputs_wide * scale_col, axis=0)
    gain_grad = lax.psum(gain_term, "dp")
    upstream = shifted(input_grad.reshape(micro_count, seq_len, feature_count), "pipe", -1)
    return (upstream[None], weight_grad[None], gain_grad[None])


def solution(mesh):
    return jax.shard_map(
        local,
        mesh=mesh,
        in_specs=(
            P("pipe", "dp", None, None),
            P("pipe", "dp", None),
            P("pipe", "dp", None),
            P("pipe", "dp", None, None),
            P("pipe", "dp", None, None),
            P("pipe", None),
            P("pipe", "dp", None),
        ),
        out_specs=(P("pipe", "dp", None, None), P("pipe", "dp", None), P("pipe", None)),
        check_vma=False,
    )
```

profile of v0, /device:TPU:0, one launch (start us, length us, event | category | flops | bytes accessed | tf_op | source)
XLA Modules:
  0.0 429.5 jit_solution(15537945578650280937)
XLA Ops:
  7.9 6.5 %copy.69 = bf16[32,8,8,1024]{3,2,1,0:T(8,128)(2,1)S(1)} copy(bf16[32,8,8,1024]{3,1,2,0:T(8,128)(2,1)} %bitcast.148) | data formatting | bytes 8388608
  14.4 2.3 copy.46
  16.7 100.3 %all_to_all.41 = bf16[256,8,1024]{2,0,1:T(8,128)(2,1)} all-to-all(bf16[256,8,1024]{2,0,1:T(8,128)(2,1)S(1)} %copy.46), channel_id=1, replica_groups=mesh['pipe'=8,'dp'=4] {'pipe'}, dimensions={1} | all-to-all | bytes 8388608 | tf_op jit(solution)/shard_map/all_to_all | solution.py:65
  117.1 4.7 %rev.3 = bf16[8,256,1024]{2,1,0:T(8,128)(2,1)} reverse(bf16[8,256,1024]{2,1,0:T(8,128)(2,1)} %bitcast.142), dimensions={0} | reverse | bytes 8388608 | tf_op jit(solution)/shard_map/rev | solution.py:66
  121.7 5.2 %all-to-all-start.1 = ((bf16[8,256,1024]{2,1,0:T(8,128)(2,1)}), bf16[8,256,1024]{2,1,0:T(8,128)(2,1)}, u32[]{:S(2)}, u32[]{:S(2)}) async-start(bf16[8,256,1024]{2,1,0:T(8,128)(2,1)} %rev.3), calls=%async_computation.1 | async-start | bytes 8388608 | tf_op jit(solution)/shard_map/all_to_all | solution.py:67
  127.0 2.2 copy.70
  129.3 1.8 copy.71
  131.3 88.1 %all-to-all-done.1 = bf16[8,256,1024]{2,1,0:T(8,128)(2,1)} async-done(((bf16[8,256,1024]{2,1,0:T(8,128)(2,1)}), bf16[8,256,1024]{2,1,0:T(8,128)(2,1)}, u32[]{:S(2)}, u32[]{:S(2)}) %all-to-all-start.1) | async-done | bytes 4194336 | tf_op jit(solution)/shard_map/all_to_all | solution.py:67
  219.4 6.5 %copy.47 = bf16[1,256,8,1024]{3,2,1,0:T(8,128)(2,1)} copy(bf16[1,256,8,1024]{3,1,2,0:T(8,128)(2,1)} %bitcast.3) | data formatting | bytes 8388608 | tf_op jit(solution)/shard_map/all_to_all | solution.py:67
  225.9 7.4 %reshape.137 = bf16[2,128,8192]{2,1,0:T(8,128)(2,1)} reshape(bf16[1,256,8,1024]{3,2,1,0:T(8,128)(2,1)} %copy.47) | data formatting | bytes 8388608 | tf_op jit(solution)/shard_map/reshape | solution.py:67
  233.3 4.7 %fusion.71 = (bf16[2,128,4096]{2,1,0:T(8,128)(2,1)}, bf16[2,128,4096]{2,1,0:T(8,128)(2,1)}) fusion(bf16[2,128,8192]{2,1,0:T(8,128)(2,1)} %reshape.137), kind=kLoop, calls=%fused_computation.79 | loop fusion | bytes 8388608 | tf_op jit(solution)/shard_map/jit(_take)/gather | solution.py:70
  238.1 3.6 gather_fusion
  241.6 3.6 gather_fusion.1
  245.2 3.3 constant_dynamic-update-slice_fusion.1
  250.0 7.8 %gather.10 = bf16[256,4,2048]{2,1,0:T(4,128)(2,1)} reshape(bf16[2,128,8192]{2,1,0:T(8,128)(2,1)} %constant_dynamic-update-slice_fusion) | data formatting | bytes 8388608 | tf_op jit(solution)/shard_map/jit(_take)/gather | solution.py:70
  257.8 4.2 broadcast_select_fusion
  262.0 4.3 copy.58
  266.3 4.8 %all-to-all-start.2 = ((bf16[256,4,2048]{2,0,1:T(8,128)(2,1)}), bf16[256,4,2048]{2,0,1:T(8,128)(2,1)}, u32[]{:S(2)}, u32[]{:S(2)}) async-start(bf16[256,4,2048]{2,0,1:T(8,128)(2,1)} %copy.58), calls=%async_computation.2 | async-start | bytes 8388608 | tf_op jit(solution)/shard_map/all_to_all | solution.py:79
  271.4 3.4 multiply_reduce_fusion
  274.8 4.7 %bitcast_select_fusion.1 = bf16[256,8192]{1,0:T(8,128)(2,1)} fusion(bf16[2,128,8192]{2,1,0:T(8,128)(2,1)} %constant_dynamic-update-slice_fusion, pred[256]{0:T(512)(128)(4,1)S(1)} %broadcast_bitcast_fusion), kind=kLoop, calls=%fused_computation.30 | loop fusion | flops 2097152 | bytes 8388864 | tf_op jit(solution)/shard_map/jit(_take)/select_n | solution.py:70
  279.5 11.6 %fusion.36 = bf16[256,1024]{1,0:T(8,128)(2,1)S(1)} fusion(bf16[1,8192,1024]{2,1,0:T(8,128)(2,1)} %all-gather.7.cloned.1.call-done, bf16[256,8192]{1,0:T(8,128)(2,1)} %bitcast_select_fusion.1, f32[8192]{0:T(1024)S(1)} %bitcast.156, f32[256]{0:T(256)S(1)} %get-tuple-element.10), kind=kOutput, calls=%fused_computation.51 | convolution fusion | flops 4303618048 | bytes 21529600 | tf_op jit(solution)/shard_map/dot_general | solution.py:85
  294.0 3.0 fusion.31
  298.0 7.5 %fusion.62 = bf16[2,128,4,128]{3,1,2,0:T(8,128)(2,1)S(1)} fusion(bf16[2,128,4,8,128]{4,3,2,1,0:T(8,128)(2,1)S(1)} %bitcast.145, f32[2,4,128,128,8]{3,2,4,1,0:T(8,128)} %fusion.31, f32[2,4,8,128,128]{3,4,2,1,0:T(8,128)} %copy-done.7, f32[2,4,8,128]{3,2,1,0:T(8,128)S(1)} %get-tuple-element.11), kind=kOutput, calls=%fused_computation.57 | convolution fusion | flops 275914880 | bytes 10780672 | tf_op jit(solution)/shard_map/bhgqk,bqhgd->bkhd/dot_general | solution.py:51
  306.1 10.4 %fusion.13 = (f32[8192]{0:T(1024)S(1)}, f32[256]{0:T(256)S(1)}, f32[256,8192]{1,0:T(8,128)S(1)}) fusion(bf16[256,8192]{1,0:T(8,128)(2,1)} %bitcast_select_fusion.1, f32[256]{0:T(256)S(1)} %get-tuple-element.10, f32[8192]{0:T(1024)S(1)} %bitcast.157, bf16[256,1024]{1,0:T(8,128)(2,1)S(1)} %bitcast_dynamic-update-slice_fusion, ...), kind=kOutput, calls=%fused_computation.19 | convolution fusion | flops 4309639168 | bytes 29952000 | tf_op jit(solution)/shard_map/dot_general | solution.py:100
  316.5 6.2 %fusion.10 = bf16[256,8192]{1,0:T(8,128)(2,1)} fusion(f32[256,8192]{1,0:T(8,128)S(1)} %get-tuple-element.13, f32[256]{0:T(256)S(1)} %broadcast_multiply_fusion, f32[256]{0:T(256)S(1)} %multiply_multiply_fusion, f32[8192]{0:T(1024)S(1)} %bitcast.158, f32[256]{0:T(256)S(1)} %get-tuple-element.10, bf16[2,128,8192]{2,1,0:T(8,128)(2,1)} %constant_dynamic-update-slice_fusion, ...), kind=kLoop, calls=%fused_computation.16 | loop fusion | flops 16777216 | bytes 16813312 | tf_op jit(solution)/shard_map/convert_element_type | solution.py:108
  324.0 5.1 %all-gather.1 = f32[4,1,256]{2,1,0:T(1,128)S(1)} all-gather(f32[1,1,256]{2,1,0:T(1,128)S(1)} %bitcast.163), channel_id=1, replica_groups=mesh['pipe'=8,'dp'=4] {'dp'}, dimensions={0}, use_global_device_ids=true | all-gather | bytes 5120 | tf_op jit(solution)/shard_map/all_gather | solution.py:80
  329.1 5.2 %fusion.15 = bf16[1024,2048]{1,0:T(8,128)(2,1)} fusion(f32[2048]{0:T(1024)S(1)} %bitcast.159, f32[1024]{0:T(1024)S(1)} %bitcast.161, bf16[256,4,2048]{2,0,1:T(8,128)(2,1)} %all-to-all-done.2), kind=kLoop, calls=%fused_computation.22 | loop fusion | flops 8388608 | bytes 8400896 | tf_op jit(solution)/shard_map/convert_element_type | solution.py:82
  334.2 14.2 %psum.7 = f32[1,8192]{1,0:T(1,128)} all-reduce(f32[1,8192]{1,0:T(1,128)S(1)} %bitcast.160), channel_id=1, replica_groups=mesh['pipe'=8,'dp'=4] {'dp'}, use_global_device_ids=true, to_apply=%region_6.7 | all-reduce | flops 8192 | bytes 65536 | tf_op jit(solution)/shard_map/psum | solution.py:110
  348.4 2.2 all-gather.5.cloned.1.call-done
  350.7 9.4 %convert_bitcast_fusion = bf16[1,2048,1024]{2,1,0:T(8,128)(2,1)} fusion(bf16[1024,2048]{1,0:T(8,128)(2,1)} %fusion.15, bf16[1024,1024]{1,0:T(8,128)(2,1)} %all-gather.5.cloned.1.call-done), kind=kOutput, calls=%fused_computation.31 | convolution fusion | flops 4297064448 | bytes 10485760 | tf_op jit(solution)/shard_map/dot_general | solution.py:97
  360.1 57.6 %collective-permute-done = bf16[2,128,8192]{2,1,0:T(8,128)(2,1)} collective-permute-done((bf16[2,128,8192]{2,1,0:T(8,128)(2,1)}, bf16[2,128,8192]{2,1,0:T(8,128)(2,1)}, u32[]{:S(2)}, u32[]{:S(2)}) %collective-permute-start) | collective-permute-done | bytes 4194336 | tf_op jit(solution)/shard_map/ppermute | solution.py:19
  417.7 4.6 %copy.99 = bf16[1,2,128,8192]{3,2,1,0:T(8,128)(2,1)} copy(bf16[1,2,128,8192]{3,2,1,0:T(8,128)(2,1)} %bitcast.26) | data formatting | bytes 8388608
  (45 shorter events, 8.4 us)
Async XLA Ops:
  7.2 272.3 %all-gather.7.cloned.1.call-start = ((), (), s32[]{:S(2)}) async-start(), calls=%async_computation.4 | async-start | bytes 20971520 | tf_op jit(solution)/shard_map/all_gather | solution.py:84
  121.7 5.2 %copy-start.4 = (bf16[1,8192]{1,0:T(2,128)(2,1)S(1)}, bf16[1,8192]{1,0:T(2,128)(2,1)}, u32[]{:S(2)}) copy-start(bf16[1,8192]{1,0:T(2,128)(2,1)} %param.12) | copy-start | bytes 49156
  121.7 97.7 %all-to-all-start.1 = ((bf16[8,256,1024]{2,1,0:T(8,128)(2,1)}), bf16[8,256,1024]{2,1,0:T(8,128)(2,1)}, u32[]{:S(2)}, u32[]{:S(2)}) async-start(bf16[8,256,1024]{2,1,0:T(8,128)(2,1)} %rev.3), calls=%async_computation.1 | async-start | bytes 8388608 | tf_op jit(solution)/shard_map/all_to_all | solution.py:67
  127.0 2.3 copy-start.2
  127.0 4.1 copy-start.6
  127.0 4.2 copy-start.5
  245.2 3.3 copy-start.1
  266.3 62.8 %all-to-all-start.2 = ((bf16[256,4,2048]{2,0,1:T(8,128)(2,1)}), bf16[256,4,2048]{2,0,1:T(8,128)(2,1)}, u32[]{:S(2)}, u32[]{:S(2)}) async-start(bf16[256,4,2048]{2,0,1:T(8,128)(2,1)} %copy.58), calls=%async_computation.2 | async-start | bytes 8388608 | tf_op jit(solution)/shard_map/all_to_all | solution.py:79
  271.1 79.5 %all-gather.5.cloned.1.call-start = ((), (), s32[]{:S(2)}) async-start(), calls=%async_computation.3 | async-start | bytes 2621440 | tf_op jit(solution)/shard_map/all_gather | solution.py:96
  292.4 1.6 copy-start
  293.8 3.2 copy-start.7
  306.1 10.4 %copy-start.3 = (bf16[256,1024]{1,0:T(8,128)(2,1)}, bf16[256,1024]{1,0:T(8,128)(2,1)S(1)}, u32[]{:S(2)}) copy-start(bf16[256,1024]{1,0:T(8,128)(2,1)S(1)} %bitcast_dynamic-update-slice_fusion) | copy-start | bytes 1572868
  322.6 95.1 %collective-permute-start = (bf16[2,128,8192]{2,1,0:T(8,128)(2,1)}, bf16[2,128,8192]{2,1,0:T(8,128)(2,1)}, u32[]{:S(2)}, u32[]{:S(2)}) collective-permute-start(bf16[2,128,8192]{2,1,0:T(8,128)(2,1)} %bitcast.25), channel_id=1, source_target_pairs={{4,0},{8,4},{12,8},{16,12},{20,16},{24,20},{28,24},{5,1},{9,5},{13... | collective-permute-start | bytes 12582920 | tf_op jit(solution)/shard_map/ppermute | solution.py:19
Sparse Core Ops, SparseCore 0:
  9.6 108.6 all-gather.6
  324.1 26.5 all-gather.4
where the time goes:
time: 437 us; the launch traced here: 429 us
  waiting for transfers between devices  149 us (34%)
  blocking collectives  120 us (27%)
  local copies, waits for them, and re-layouts  66 us (15%)
  matrix products  43.9 us (10%)
  other arithmetic  25.2 us (6%)
  between operations  14.6 us (3%)
  starting transfers between devices  11.6 us (3%)
    all_to_all x1, blocking collectives, local(): lax.all_to_all(flat_stored, 'pipe', split_axis=1, concat_axis=0, tiled=True)  100 us
    all_to_all x1, waiting for transfers between devices, local(): lax.all_to_all(blocks, 'pipe', split_axis=0, concat_axis=2, tiled=True)  88.1 us
    ppermute x1, waiting for transfers between devices, shifted(): lax.ppermute(value, axis, [(source, source + steps) for source in range(l...  57.6 us
    unnamed x25, local copies, waits for them, and re-layouts  20.5 us
    gather x4, local copies, waits for them, and re-layouts, local(): inputs = jnp.take(fetched, slot_order[0, 0], axis=0)  19.7 us
    psum x1, blocking collectives, local(): gain_grad = lax.psum(gain_term, 'dp')  14.2 us
    dot_general x1, matrix products, local(): projected = jnp.dot(normed, full_weight, preferred_element_type=jnp.float32)  11.6 us
    dot_general x1, matrix products, local(): lax.dot_general(kv_grads, full_weight, (((1,), (1,)), ((), ())), preferre...  10.4 us
  transfers between devices with their start and end apart: 5, of which 3 were waited for; matrix products, arithmetic and copies ran while one was open for 30% of the time, Pallas kernels for 0%

commit v1 on v0

v1 whole, which is shorter than its diff:
```python
import math

import jax
import jax.numpy as jnp
from jax import lax
from jax.sharding import PartitionSpec as P

QH = 32
KVH = 4
HD = 128


EPSILON = 1e-05


def shifted(value, axis, steps):
    count = lax.axis_size(axis)
    leading, last = (max(0, -steps), min(count, count - steps))
    return lax.ppermute(value, axis, [(source, source + steps) for source in range(leading, last)])


def mirrored(value, axis):
    count = lax.axis_size(axis)
    return lax.ppermute(value, axis, [(source, count - 1 - source) for source in range(count)])


def attention_grads(queries, out_grad, keys, values, segments):
    seq_len = queries.shape[0]
    group_size = QH // KVH
    scaling = 1.0 / math.sqrt(HD)
    query_heads = queries.reshape(seq_len, KVH, group_size, HD)
    grad_heads = out_grad.reshape(seq_len, KVH, group_size, HD)
    key_heads = keys.reshape(seq_len, KVH, HD)
    value_heads = values.reshape(seq_len, KVH, HD)
    scores = (
        jnp.einsum("qhgd,khd->hgqk", query_heads, key_heads, preferred_element_type=jnp.float32)
        * scaling
    )
    position = jnp.arange(seq_len)
    causal = position[None, :] <= position[:, None]
    allowed = causal & (segments[:, None] == segments[None, :])
    scores = jnp.where(allowed[None, None], scores, -1e30)
    highest = jnp.max(scores, axis=-1, keepdims=True)
    weights = jnp.exp(scores - highest)
    probabilities = weights / jnp.sum(weights, axis=-1, keepdims=True)
    probs_low = probabilities.astype(jnp.bfloat16)
    value_grad = jnp.einsum(
        "hgqk,qhgd->khd", probs_low, grad_heads, preferred_element_type=jnp.float32
    )
    prob_grad = jnp.einsum(
        "qhgd,khd->hgqk", grad_heads, value_heads, preferred_element_type=jnp.float32
    )
    row_dot = jnp.sum(probabilities * prob_grad, axis=-1, keepdims=True)
    score_grad = (probabilities * (prob_grad - row_dot) * scaling).astype(jnp.bfloat16)
    key_grad = jnp.einsum(
        "hgqk,qhgd->khd", score_grad, query_heads, preferred_element_type=jnp.float32
    )
    key_low = key_grad.astype(jnp.bfloat16).reshape(seq_len, KVH * HD)
    value_low = value_grad.astype(jnp.bfloat16).reshape(seq_len, KVH * HD)
    return jnp.concatenate([key_low, value_low], axis=-1)


def local(parked, slot_order, segment_ids, queries, out_grad, norm_gain, kv_weight):
    stored = parked[0]
    order = slot_order[0, 0]
    micro_count, seq_len, feature_count = stored.shape
    gain_full = norm_gain[0].astype(jnp.float32)
    local_weight = kv_weight[0]
    slice_width = local_weight.shape[0]
    start_col = lax.axis_index("dp") * slice_width
    gain_local = lax.dynamic_slice_in_dim(gain_full, start_col, slice_width)
    full_weight = lax.all_gather(local_weight, "dp", axis=0, tiled=True)
    order_next = shifted(order, "pipe", -1)

    arrived = []
    for slot in range(micro_count):
        block = stored[slot]
        if arrived:
            arrived[-1], block = lax.optimization_barrier((arrived[-1], block))
        arrived.append(mirrored(block, "pipe"))

    all_normed, all_grads, shifts = [], [], []
    for slot in range(micro_count):
        micro = jnp.argmax(order == slot)
        inputs_wide = arrived[slot].astype(jnp.float32)
        inverse = lax.rsqrt(jnp.mean(inputs_wide * inputs_wide, axis=-1, keepdims=True) + EPSILON)
        normed = (inputs_wide * inverse * gain_full).astype(jnp.bfloat16)
        all_normed.append(lax.all_to_all(normed, "dp", split_axis=1, concat_axis=0, tiled=True))
        projected = jnp.dot(normed, full_weight, preferred_element_type=jnp.float32)
        projected_low = projected.astype(jnp.bfloat16)
        head_span = projected_low.shape[-1] // 2
        kv_grads = attention_grads(
            lax.dynamic_index_in_dim(queries[0], micro, keepdims=False),
            lax.dynamic_index_in_dim(out_grad[0], micro, keepdims=False),
            projected_low[..., :head_span],
            projected_low[..., head_span:],
            lax.dynamic_index_in_dim(segment_ids[0], micro, keepdims=False),
        )
        all_grads.append(lax.all_gather(kv_grads, "dp", axis=0, tiled=True))
        inner = jnp.sum(kv_grads.astype(jnp.float32) * projected, axis=-1, keepdims=True)
        inner = inner * (inverse * inverse / feature_count)
        normed_grad = lax.dot_general(
            kv_grads, full_weight, (((1,), (1,)), ((), ())), preferred_element_type=jnp.float32
        )
        input_grad = (inverse * gain_full * normed_grad - inputs_wide * inner).astype(jnp.bfloat16)
        shifts.append(shifted(input_grad, "pipe", -1))
        if slot + 1 < micro_count:
            arrived[slot + 1], _ = lax.optimization_barrier((arrived[slot + 1], input_grad))

    weight_wide = lax.dot_general(
        jnp.concatenate(all_normed),
        jnp.concatenate(all_grads),
        (((0,), (0,)), ((), ())),
        preferred_element_type=jnp.float32,
    )
    gain_part = jnp.sum(weight_wide * local_weight.astype(jnp.float32), axis=-1) / gain_local
    gain_grad = lax.all_gather(gain_part, "dp", axis=0, tiled=True)
    upstream = jnp.zeros((micro_count, seq_len, feature_count), jnp.bfloat16)
    for slot in range(micro_count):
        upstream = lax.dynamic_update_index_in_dim(
            upstream, shifts[slot], jnp.argmax(order_next == slot), 0
        )
    return (upstream[None], weight_wide.astype(jnp.bfloat16)[None], gain_grad[None])


def solution(mesh):
    return jax.shard_map(
        local,
        mesh=mesh,
        in_specs=(
            P("pipe", "dp", None, None),
            P("pipe", "dp", None),
            P("pipe", "dp", None),
            P("pipe", "dp", None, None),
            P("pipe", "dp", None, None),
            P("pipe", None),
            P("pipe", "dp", None),
        ),
        out_specs=(P("pipe", "dp", None, None), P("pipe", "dp", None), P("pipe", None)),
        check_vma=False,
    )
```

time: 437 us -> 354 us (0.81)
  the two profiles are of different devices: /device:TPU:0 before, /device:TPU:14 now
where the time goes in v1:
time: 354 us; the launch traced here: 352 us
  waiting for transfers between devices  170 us (48%)
  matrix products  79.2 us (22%)
  local copies, waits for them, and re-layouts  42.2 us (12%)
  between operations  21.7 us (6%)
  starting transfers between devices  21.2 us (6%)
  other arithmetic  12.6 us (4%)
  blocking collectives  5.18 us (1%)
    ppermute x2, waiting for transfers between devices, mirrored(): lax.ppermute(value, axis, [(source, count - 1 - source) for source in ran...  126 us
    dot_general x2, matrix products, local(): lax.dot_general(kv_grads, full_weight, (((1,), (1,)), ((), ())), preferre...  26.3 us
    ppermute x3, waiting for transfers between devices, shifted(): lax.ppermute(value, axis, [(source, source + steps) for source in range(l...  24.5 us
    unnamed x37, local copies, waits for them, and re-layouts  22.7 us
    all_to_all x2, waiting for transfers between devices, local(): lax.all_to_all(normed, 'dp', split_axis=1, concat_axis=0, tiled=True)  19.4 us
    dot_general x2, matrix products, local(): projected = jnp.dot(normed, full_weight, preferred_element_type=jnp.float32)  18 us
    all_to_all x2, starting transfers between devices, local(): lax.all_to_all(normed, 'dp', split_axis=1, concat_axis=0, tiled=True)  11.2 us
    dot_general x1, matrix products, local(): lax.dot_general(jnp.concatenate(all_normed), jnp.concatenate(all_grads),...  11 us
  transfers between devices with their start and end apart: 10, of which 5 were waited for; matrix products, arithmetic and copies ran while one was open for 29% of the time, Pallas kernels for 0%

profile of v1, /device:TPU:14, one launch (start us, length us, event | category | flops | bytes accessed | tf_op | source)
XLA Modules:
  0.0 352.3 jit_solution(518130009902933756)
XLA Ops:
  8.0 4.7 %slice_bitcast_fusion = (bf16[128,8192]{1,0:T(8,128)(2,1)}, bf16[128,8192]{1,0:T(8,128)(2,1)}) fusion(bf16[1,2,128,8192]{3,2,1,0:T(8,128)(2,1)} %param.7), kind=kLoop, calls=%fused_computation.58 | loop fusion | bytes 8388608 | tf_op jit(solution)/shard_map/squeeze | solution.py:77
  19.4 4.7 %constant_dynamic-slice_fusion.1 = (bf16[1,1,128,4096]{3,2,1,0:T(8,128)(2,1)}, bf16[1,1,128,4096]{3,2,1,0:T(8,128)(2,1)S(1)}, bf16[1,1,128,4096]{3,2,1,0:T(8,128)(2,1)}, bf16[1,1,128,4096]{3,2,1,0:T(8,128)(2,1)}) fusion(bf16[1,2,128,4096]{3,2,1,0:T(8,128)(2,1)} %param.11, s32[]{:T(128)S(6)} %select_n.42, s32[]{:T(128)S(6)} %select_n.39, ...), kind=kLoop, calls=%fused_computation.102 | loop fusion | bytes 8388616 | tf_op jit(solution)/shard_map/jit(dynamic_index_in_dim)/dynamic_slice | solution.py:94
  24.1 2.4 copy.104
  29.5 2.3 copy.106
  31.9 119.1 %collective-permute-done = bf16[128,8192]{1,0:T(8,128)(2,1)S(1)} collective-permute-done((bf16[128,8192]{1,0:T(8,128)(2,1)}, bf16[128,8192]{1,0:T(8,128)(2,1)S(1)}, u32[]{:S(2)}, u32[]{:S(2)}) %collective-permute-start) | collective-permute-done | bytes 2097184 | tf_op jit(solution)/shard_map/ppermute | solution.py:24
  153.1 2.2 fusion.21
  156.7 8.9 %fusion.103 = (bf16[128,1024]{1,0:T(8,128)(2,1)S(1)}, f32[128,1024]{1,0:T(8,128)}) fusion(bf16[128,8192]{1,0:T(8,128)(2,1)S(1)} %fusion.21, bf16[1,8192,1024]{2,1,0:T(8,128)(2,1)} %all-gather.9.cloned.1.call-done), kind=kOutput, calls=%fused_computation.129 | convolution fusion | flops 2147614720 | bytes 19660800 | tf_op jit(solution)/shard_map/dot_general | solution.py:89
  167.3 3.3 fusion.104
  170.7 3.4 fusion.54
  174.1 3.2 fusion.52
  179.5 12.8 %fusion.23 = bf16[128,8192]{1,0:T(8,128)(2,1)} fusion(bf16[128,8192]{1,0:T(8,128)(2,1)S(1)} %copy-done.1, bf16[1,8192,1024]{2,1,0:T(8,128)(2,1)} %all-gather.9.cloned.1.call-done, f32[128]{0:T(128)S(1)} %multiply_multiply_fusion.1, f32[8192]{0:T(1024)S(1)} %bitcast.175, f32[128]{0:T(128)S(1)} %add_rsqrt_fusion.1, bf16[128,512]{1,0:T(8,128)(2,1)S(1)} %copy.97, ...), kind=kOutput, calls=%fused_computation.26 | convolution fusion | flops 2154299392 | bytes 21267456 | tf_op jit(solution)/shard_map/dot_general | solution.py:102
  192.4 6.6 %collective-permute-done.3 = bf16[128,8192]{1,0:T(8,128)(2,1)} collective-permute-done((bf16[128,8192]{1,0:T(8,128)(2,1)}, bf16[128,8192]{1,0:T(8,128)(2,1)}, u32[]{:S(2)}, u32[]{:S(2)}) %collective-permute-start.3) | collective-permute-done | bytes 2097184 | tf_op jit(solution)/shard_map/ppermute | solution.py:24
  199.0 2.1 fusion.24
  201.1 2.2 fusion.26
  203.3 9.1 %fusion.107 = (bf16[128,1024]{1,0:T(8,128)(2,1)S(1)}, f32[128,1024]{1,0:T(8,128)}) fusion(bf16[128,8192]{1,0:T(8,128)(2,1)S(1)} %fusion.26, bf16[1,8192,1024]{2,1,0:T(8,128)(2,1)} %all-gather.9.cloned.1.call-done), kind=kOutput, calls=%fused_computation.131 | convolution fusion | flops 2147614720 | bytes 19660800 | tf_op jit(solution)/shard_map/dot_general | solution.py:89
  217.4 4.0 %fusion.108 = (f32[4,8,128]{2,1,0:T(8,128)}, f32[4,8,128,128]{2,3,1,0:T(8,128)}) fusion(pred[128,128]{0,1:T(8,128)(4,1)S(1)} %get-tuple-element.50, bf16[128,4,8,128]{0,3,2,1:T(8,128)(2,1)} %bitcast.168, bf16[128,4,128,1]{2,1,0,3:T(4,128)(2,1)} %bitcast.181), kind=kOutput, calls=%fused_computation.132 | convolution fusion | flops 136315008 | bytes 3309568 | tf_op jit(solution)/shard_map/sub | solution.py:44
  221.4 2.1 fusion.53
  223.5 4.6 %fusion.55 = bf16[4,128,128]{2,1,0:T(8,128)(2,1)S(1)} fusion(bf16[128,4,8,128]{0,3,2,1:T(8,128)(2,1)} %bitcast.169, f32[4,128,128,8]{2,1,3,0:T(8,128)} %fusion.68, f32[4,8,128,128]{2,3,1,0:T(8,128)} %get-tuple-element.47, f32[4,8,128]{2,1,0:T(8,128)S(1)} %copy-done.14), kind=kOutput, calls=%fused_computation.71 | convolution fusion | flops 137957504 | bytes 5390336 | tf_op jit(solution)/shard_map/hgqk,qhgd->khd/dot_general | solution.py:55
  229.1 5.0 %all-to-all-start = ((bf16[128,4,2048]{2,0,1:T(8,128)(2,1)}), bf16[128,4,2048]{2,0,1:T(8,128)(2,1)}, u32[]{:S(2)}, u32[]{:S(2)}) async-start(bf16[128,4,2048]{2,0,1:T(8,128)(2,1)} %bitcast.162), calls=%async_computation | async-start | bytes 4194304 | tf_op jit(solution)/shard_map/all_to_all | solution.py:88
  234.1 2.4 collective-permute-start.2
  236.5 6.5 %copy.74 = bf16[1,2048,1024]{1,2,0:T(8,128)(2,1)} copy(bf16[1,2048,1024]{2,1,0:T(8,128)(2,1)} %param.13) | data formatting | bytes 8388608 | tf_op args[6]
  248.2 1.9 collective-permute-start.1
  252.3 11.5 %all-to-all-done = bf16[128,4,2048]{2,0,1:T(8,128)(2,1)} async-done(((bf16[128,4,2048]{2,0,1:T(8,128)(2,1)}), bf16[128,4,2048]{2,0,1:T(8,128)(2,1)}, u32[]{:S(2)}, u32[]{:S(2)}) %all-to-all-start) | async-done | bytes 2097184 | tf_op jit(solution)/shard_map/all_to_all | solution.py:88
  263.9 6.2 %all-to-all-start.1 = ((bf16[128,4,2048]{2,0,1:T(8,128)(2,1)}), bf16[128,4,2048]{2,0,1:T(8,128)(2,1)}, u32[]{:S(2)}, u32[]{:S(2)}) async-start(bf16[128,4,2048]{2,0,1:T(8,128)(2,1)} %bitcast.163), calls=%async_computation.1 | async-start | bytes 4194304 | tf_op jit(solution)/shard_map/all_to_all | solution.py:88
  270.2 13.4 %fusion.28 = bf16[128,8192]{1,0:T(8,128)(2,1)} fusion(bf16[128,8192]{1,0:T(8,128)(2,1)} %collective-permute-done.3, bf16[1,8192,1024]{2,1,0:T(8,128)(2,1)} %all-gather.9.cloned.1.call-done, f32[128]{0:T(128)S(1)} %multiply_multiply_fusion, f32[128]{0:T(128)S(1)} %copy-done.9, f32[8192]{0:T(1024)S(1)} %bitcast.177, bf16[128,512]{1,0:T(8,128)(2,1)S(1)} %copy.103, ...), kind=kOutput, calls=%fused_computation.31 | convolution fusion | flops 2154299392 | bytes 21267456 | tf_op jit(solution)/shard_map/dot_general | solution.py:102
  283.7 2.6 collective-permute-start.4
  286.3 7.9 %all-to-all-done.1 = bf16[128,4,2048]{2,0,1:T(8,128)(2,1)} async-done(((bf16[128,4,2048]{2,0,1:T(8,128)(2,1)}), bf16[128,4,2048]{2,0,1:T(8,128)(2,1)}, u32[]{:S(2)}, u32[]{:S(2)}) %all-to-all-start.1) | async-done | bytes 2097184 | tf_op jit(solution)/shard_map/all_to_all | solution.py:88
  294.2 11.0 %fusion.18 = (f32[2048]{0:T(1024)S(1)}, bf16[1,2048,1024]{1,2,0:T(8,128)(2,1)}) fusion(bf16[1,2048,1024]{1,2,0:T(8,128)(2,1)} %copy.74, bf16[512,1024]{1,0:T(8,128)(2,1)} %all-gather.7.cloned.1.call-done, bf16[512,1024]{1,0:T(8,128)(2,1)} %all-gather.5.cloned.1.call-done, bf16[512,2048]{1,0:T(8,128)(2,1)} %bitcast.40, bf16[512,2048]{1,0:T(8,128)(2,1)} %bitcast.38), kind=kOutput, calls=%fused_computation.15 | convolution fusion | flops 4315936768 | bytes 14688256 | tf_op jit(solution)/shard_map/dot_general | solution.py:110
  305.2 6.4 %copy.75 = bf16[1,2048,1024]{2,1,0:T(8,128)(2,1)} copy(bf16[1,2048,1024]{1,2,0:T(8,128)(2,1)} %get-tuple-element.27) | data formatting | bytes 8388608
  311.6 5.2 %all_gather.15 = f32[8192]{0:T(1024)S(1)} all-gather(f32[2048]{0:T(1024)S(1)} %div.39), channel_id=1, replica_groups=mesh['pipe'=8,'dp'=4] {'dp'}, dimensions={0}, use_global_device_ids=true | all-gather | bytes 40960 | tf_op jit(solution)/shard_map/all_gather | solution.py:117
  317.2 1.9 bitcast_dynamic-update-slice_fusion.1
  319.1 24.4 %collective-permute-done.4 = bf16[128,8192]{1,0:T(8,128)(2,1)S(1)} collective-permute-done((bf16[128,8192]{1,0:T(8,128)(2,1)}, bf16[128,8192]{1,0:T(8,128)(2,1)S(1)}, u32[]{:S(2)}, u32[]{:S(2)}) %collective-permute-start.4) | collective-permute-done | bytes 2097184 | tf_op jit(solution)/shard_map/ppermute | solution.py:19
  (80 shorter events, 26.9 us)
Async XLA Ops:
  7.2 149.5 %all-gather.9.cloned.1.call-start = ((), (), s32[]{:S(2)}) async-start(), calls=%async_computation.4 | async-start | bytes 20971520 | tf_op jit(solution)/shard_map/all_gather | solution.py:72
  7.9 6.3 %copy-start.12 = (s32[1,1,2]{2,1,0:T(1,128)S(1)}, s32[1,1,2]{2,1,0:T(1,128)}, u32[]{:S(2)}) copy-start(s32[1,1,2]{2,1,0:T(1,128)} %param.8) | copy-start | bytes 28
  7.9 10.2 %copy-start.6 = (bf16[1,8192]{1,0:T(2,128)(2,1)S(1)}, bf16[1,8192]{1,0:T(2,128)(2,1)}, u32[]{:S(2)}) copy-start(bf16[1,8192]{1,0:T(2,128)(2,1)} %param.12) | copy-start | bytes 49156
  7.9 278.4 %all-gather.7.cloned.1.call-start = ((), (), s32[]{:S(2)}) async-start(), calls=%async_computation.3 | async-start | bytes 1310720 | tf_op jit(solution)/shard_map/all_gather | solution.py:99
  12.6 138.4 %collective-permute-start = (bf16[128,8192]{1,0:T(8,128)(2,1)}, bf16[128,8192]{1,0:T(8,128)(2,1)S(1)}, u32[]{:S(2)}, u32[]{:S(2)}) collective-permute-start(bf16[128,8192]{1,0:T(8,128)(2,1)} %get-tuple-element.29), channel_id=1, source_target_pairs={{0,28},{4,24},{8,20},{12,16},{16,12},{20,8},{24,4},{28,0},{1,29},{... | collective-permute-start | bytes 6291464 | tf_op jit(solution)/shard_map/ppermute | solution.py:24
  18.1 182.9 %copy-start.4 = (f32[1,8192]{1,0:T(1,128)}, f32[1,8192]{1,0:T(1,128)S(1)}, u32[]{:S(2)}) copy-start(f32[1,8192]{1,0:T(1,128)S(1)} %mul.192) | copy-start | bytes 98308
  27.8 4.0 %copy-start.7 = (s32[1,2,128]{2,1,0:T(2,128)S(1)}, s32[1,2,128]{2,1,0:T(2,128)}, u32[]{:S(2)}) copy-start(s32[1,2,128]{2,1,0:T(2,128)} %param.9) | copy-start | bytes 3076
  151.0 2.0 copy-start
  151.0 48.0 %collective-permute-start.3 = (bf16[128,8192]{1,0:T(8,128)(2,1)}, bf16[128,8192]{1,0:T(8,128)(2,1)}, u32[]{:S(2)}, u32[]{:S(2)}) collective-permute-start(bf16[128,8192]{1,0:T(8,128)(2,1)} %get-tuple-element.13), channel_id=1, source_target_pairs={{0,28},{4,24},{8,20},{12,16},{16,12},{20,8},{24,4},{28,0},{1,29},{... | collective-permute-start | bytes 6291464 | tf_op jit(solution)/shard_map/ppermute | solution.py:24
  174.1 5.4 %copy-start.1 = (bf16[128,8192]{1,0:T(8,128)(2,1)S(1)}, bf16[128,8192]{1,0:T(8,128)(2,1)}, u32[]{:S(2)}) copy-start(bf16[128,8192]{1,0:T(8,128)(2,1)} %copy-done) | copy-start | bytes 6291460
  201.0 2.2 copy-start.10
  201.1 2.2 copy-start.8
  221.4 2.1 copy-start.14
  229.1 5.0 %copy-start.13 = (s32[1,1,2]{2,1,0:T(1,128)S(1)}, s32[1,1,2]{2,1,0:T(1,128)}, u32[]{:S(2)}) copy-start(s32[1,1,2]{2,1,0:T(1,128)} %param.8) | copy-start | bytes 28
  229.1 34.7 %all-to-all-start = ((bf16[128,4,2048]{2,0,1:T(8,128)(2,1)}), bf16[128,4,2048]{2,0,1:T(8,128)(2,1)}, u32[]{:S(2)}, u32[]{:S(2)}) async-start(bf16[128,4,2048]{2,0,1:T(8,128)(2,1)} %bitcast.162), calls=%async_computation | async-start | bytes 4194304 | tf_op jit(solution)/shard_map/all_to_all | solution.py:88
  234.1 52.2 %all-gather.5.cloned.1.call-start = ((), (), s32[]{:S(2)}) async-start(), calls=%async_computation.2 | async-start | bytes 1310720 | tf_op jit(solution)/shard_map/all_gather | solution.py:99
  234.1 8.9 %copy-start.5 = (f32[1,8192]{1,0:T(1,128)S(1)}, f32[1,8192]{1,0:T(1,128)}, u32[]{:S(2)}) copy-start(f32[1,8192]{1,0:T(1,128)} %copy-done.4) | copy-start | bytes 98308
  234.1 8.9 %collective-permute-start.2 = (s32[2]{0:T(128)S(1)}, s32[2]{0:T(128)S(1)}, u32[]{:S(2)}, u32[]{:S(2)}) collective-permute-start(s32[2]{0:T(128)S(1)} %bitcast.186), channel_id=1, source_target_pairs={{4,0},{8,4},{12,8},{16,12},{20,16},{24,20},{28,24},{5,1},{9,5},{13... | collective-permute-start | bytes 32 | tf_op jit(solution)/shard_map/ppermute | solution.py:19
  248.2 68.6 %collective-permute-start.1 = (bf16[128,8192]{1,0:T(8,128)(2,1)}, bf16[128,8192]{1,0:T(8,128)(2,1)}, u32[]{:S(2)}, u32[]{:S(2)}) collective-permute-start(bf16[128,8192]{1,0:T(8,128)(2,1)} %fusion.23), channel_id=1, source_target_pairs={{4,0},{8,4},{12,8},{16,12},{20,16},{24,20},{28,24},{5,1},{9,5},{13... | collective-permute-start | bytes 6291464 | tf_op jit(solution)/shard_map/ppermute | solution.py:19
  263.8 6.2 %copy-start.3 = (f32[128,1024]{1,0:T(8,128)S(1)}, f32[128,1024]{1,0:T(8,128)}, u32[]{:S(2)}) copy-start(f32[128,1024]{1,0:T(8,128)} %get-tuple-element.45) | copy-start | bytes 1572868
  263.9 6.4 %copy-start.11 = (f32[128]{0:T(128)S(1)}, f32[128]{0:T(128)}, u32[]{:S(2)}) copy-start(f32[128]{0:T(128)} %copy-done.10) | copy-start | bytes 1540
  263.9 6.4 %copy-start.9 = (f32[128]{0:T(128)S(1)}, f32[128]{0:T(128)}, u32[]{:S(2)}) copy-start(f32[128]{0:T(128)} %copy-done.8) | copy-start | bytes 1540
  263.9 30.3 %all-to-all-start.1 = ((bf16[128,4,2048]{2,0,1:T(8,128)(2,1)}), bf16[128,4,2048]{2,0,1:T(8,128)(2,1)}, u32[]{:S(2)}, u32[]{:S(2)}) async-start(bf16[128,4,2048]{2,0,1:T(8,128)(2,1)} %bitcast.163), calls=%async_computation.1 | async-start | bytes 4194304 | tf_op jit(solution)/shard_map/all_to_all | solution.py:88
  283.7 59.8 %collective-permute-start.4 = (bf16[128,8192]{1,0:T(8,128)(2,1)}, bf16[128,8192]{1,0:T(8,128)(2,1)S(1)}, u32[]{:S(2)}, u32[]{:S(2)}) collective-permute-start(bf16[128,8192]{1,0:T(8,128)(2,1)} %fusion.28), channel_id=1, source_target_pairs={{4,0},{8,4},{12,8},{16,12},{20,16},{24,20},{28,24},{5,1},{9,5},{13... | collective-permute-start | bytes 6291464 | tf_op jit(solution)/shard_map/ppermute | solution.py:19
  343.8 2.0 copy-start.2
Sparse Core Ops, SparseCore 0:
  9.6 106.0 all-gather.8
  229.2 21.3 all-gather.6
  252.4 19.4 all-gather.4

commit v2 on v1

--- a/solution.py
+++ b/solution.py
@@ -97,6 +97,8 @@
             lax.dynamic_index_in_dim(segment_ids[0], micro, keepdims=False),
         )
         all_grads.append(lax.all_gather(kv_grads, "dp", axis=0, tiled=True))
+        if shifts:
+            kv_grads, shifts[-1] = lax.optimization_barrier((kv_grads, shifts[-1]))
         inner = jnp.sum(kv_grads.astype(jnp.float32) * projected, axis=-1, keepdims=True)
         inner = inner * (inverse * inverse / feature_count)
         normed_grad = lax.dot_general(

time: 354 us -> 333 us (0.941)
  waiting for transfers between devices: 170 us -> 155 us
    ppermute x2, waiting for transfers between devices: 126 us -> 0.01 us  [mirrored(): lax.ppermute(value, axis, [(source, count - 1 - source) for source in ran...]
    ppermute x3, waiting for transfers between devices: 24.5 us -> 146 us  [shifted(): lax.ppermute(value, axis, [(source, source + steps) for source in range(l...]
    all_to_all x2, waiting for transfers between devices: 19.4 us -> 8.42 us  [local(): lax.all_to_all(normed, 'dp', split_axis=1, concat_axis=0, tiled=True)]
    unnamed x37 -> x31, local copies, waits for them, and re-layouts: 22.7 us -> 23.6 us
  transfers between devices with their start and end apart: 10 -> 10, of which waited for: 5 -> 4; matrix products, arithmetic and copies ran while one was open for 29% -> 39% of each run, Pallas kernels for 0% -> 0%
where the time goes in v2:
time: 333 us; the launch traced here: 332 us
  waiting for transfers between devices  155 us (47%)
  matrix products  78.7 us (24%)
  local copies, waits for them, and re-layouts  39.5 us (12%)
  between operations  21.4 us (6%)
  starting transfers between devices  18.9 us (6%)
  other arithmetic  13.1 us (4%)
  blocking collectives  5.18 us (2%)
    ppermute x3, waiting for transfers between devices, shifted(): lax.ppermute(value, axis, [(source, source + steps) for source in range(l...  146 us
    dot_general x2, matrix products, local(): lax.dot_general(kv_grads, full_weight, (((1,), (1,)), ((), ())), preferre...  26.7 us
    unnamed x31, local copies, waits for them, and re-layouts  23.6 us
    dot_general x2, matrix products, local(): projected = jnp.dot(normed, full_weight, preferred_element_type=jnp.float32)  17.8 us
    dot_general x1, matrix products, local(): lax.dot_general(jnp.concatenate(all_normed), jnp.concatenate(all_grads),...  11 us
    all_to_all x2, starting transfers between devices, local(): lax.all_to_all(normed, 'dp', split_axis=1, concat_axis=0, tiled=True)  9.81 us
    all_to_all x2, waiting for transfers between devices, local(): lax.all_to_all(normed, 'dp', split_axis=1, concat_axis=0, tiled=True)  8.42 us
    dot_general x2, matrix products, attention_grads(): jnp.einsum('hgqk,qhgd->khd', score_grad, query_heads, preferred_element_t...  7.97 us
  transfers between devices with their start and end apart: 10, of which 4 were waited for; matrix products, arithmetic and copies ran while one was open for 39% of the time, Pallas kernels for 0%

profile of v2, /device:TPU:14, one launch (start us, length us, event | category | flops | bytes accessed | tf_op | source)
XLA Modules:
  0.0 331.8 jit_solution(5357479425193541208)
XLA Ops:
  7.9 4.7 %slice_bitcast_fusion = (bf16[128,8192]{1,0:T(8,128)(2,1)}, bf16[128,8192]{1,0:T(8,128)(2,1)}) fusion(bf16[1,2,128,8192]{3,2,1,0:T(8,128)(2,1)} %param.7), kind=kLoop, calls=%fused_computation.58 | loop fusion | bytes 8388608 | tf_op jit(solution)/shard_map/squeeze | solution.py:77
  14.2 3.4 %collective-permute-start.3 = (s32[2]{0:T(128)S(1)}, s32[2]{0:T(128)S(1)}, u32[]{:S(2)}, u32[]{:S(2)}) collective-permute-start(s32[2]{0:T(128)S(1)} %bitcast.189), channel_id=1, source_target_pairs={{4,0},{8,4},{12,8},{16,12},{20,16},{24,20},{28,24},{5,1},{9,5},{13... | collective-permute-start | bytes 32 | tf_op jit(solution)/shard_map/ppermute | solution.py:19
  21.4 6.9 %copy.74 = bf16[1,2048,1024]{1,2,0:T(8,128)(2,1)} copy(bf16[1,2048,1024]{2,1,0:T(8,128)(2,1)} %param.13) | data formatting | bytes 8388608 | tf_op args[6]
  29.5 4.1 %constant_dynamic-slice_fusion.2 = (bf16[1,1,128,4096]{3,2,1,0:T(8,128)(2,1)S(1)}, bf16[1,1,128,4096]{3,2,1,0:T(8,128)(2,1)}, bf16[1,1,128,4096]{3,2,1,0:T(8,128)(2,1)}, bf16[1,1,128,4096]{3,2,1,0:T(8,128)(2,1)}) fusion(bf16[1,2,128,4096]{3,2,1,0:T(8,128)(2,1)} %param.11, s32[]{:T(128)S(6)} %select_n.40, s32[]{:T(128)S(6)} %select_n.39, ...), kind=kLoop, calls=%fused_computation.103 | loop fusion | bytes 8388616 | tf_op jit(solution)/shard_map/jit(dynamic_index_in_dim)/dynamic_slice | solution.py:94
  33.6 2.3 copy.105
  38.9 2.3 copy.104
  41.9 109.1 %collective-permute-done.3 = s32[2]{0:T(128)S(1)} collective-permute-done((s32[2]{0:T(128)S(1)}, s32[2]{0:T(128)S(1)}, u32[]{:S(2)}, u32[]{:S(2)}) %collective-permute-start.3) | collective-permute-done | bytes 40 | tf_op jit(solution)/shard_map/ppermute | solution.py:19
  157.4 2.2 fusion.27
  161.0 4.9 %all-to-all-start = ((bf16[128,4,2048]{2,0,1:T(8,128)(2,1)}), bf16[128,4,2048]{2,0,1:T(8,128)(2,1)}, u32[]{:S(2)}, u32[]{:S(2)}) async-start(bf16[128,4,2048]{2,0,1:T(8,128)(2,1)} %bitcast.165), calls=%async_computation | async-start | bytes 4194304 | tf_op jit(solution)/shard_map/all_to_all | solution.py:88
  165.9 8.9 %fusion.105 = (bf16[128,1024]{1,0:T(8,128)(2,1)S(1)}, f32[128,1024]{1,0:T(8,128)}) fusion(bf16[128,8192]{1,0:T(8,128)(2,1)S(1)} %fusion.27, bf16[1,8192,1024]{2,1,0:T(8,128)(2,1)} %all-gather.9.cloned.1.call-done), kind=kOutput, calls=%fused_computation.129 | convolution fusion | flops 2147614720 | bytes 19660800 | tf_op jit(solution)/shard_map/dot_general | solution.py:89
  176.6 3.4 %fusion.106 = (f32[4,8,128]{2,1,0:T(8,128)S(1)}, f32[4,8,128,128]{2,3,1,0:T(8,128)}) fusion(pred[128,128]{0,1:T(8,128)(4,1)S(1)} %get-tuple-element.54, bf16[128,4,8,128]{0,3,2,1:T(8,128)(2,1)} %bitcast.173, bf16[128,4,128,1]{2,1,0,3:T(4,128)(2,1)S(1)} %bitcast.182), kind=kOutput, calls=%fused_computation.130 | convolution fusion | flops 136315008 | bytes 3309568 | tf_op jit(solution)/shard_map/sub | solution.py:44
  180.0 3.4 %fusion.56 = bf16[4,128,128]{2,1,0:T(8,128)(2,1)S(1)} fusion(bf16[128,4,8,128]{0,3,2,1:T(8,128)(2,1)} %bitcast.174, f32[4,128,128,8]{2,1,3,0:T(8,128)S(1)} %fusion.74, f32[4,8,128,128]{2,3,1,0:T(8,128)} %get-tuple-element.47, f32[4,8,128]{2,1,0:T(8,128)S(1)} %get-tuple-element.46), kind=kOutput, calls=%fused_computation.70 | convolution fusion | flops 137957504 | bytes 5390336 | tf_op jit(solution)/shard_map/hgqk,qhgd->khd/dot_general | solution.py:55
  183.5 3.2 fusion.54
  189.9 13.1 %fusion.29 = bf16[128,8192]{1,0:T(8,128)(2,1)} fusion(bf16[128,8192]{1,0:T(8,128)(2,1)S(1)} %copy-done.1, bf16[1,8192,1024]{2,1,0:T(8,128)(2,1)} %all-gather.9.cloned.1.call-done, f32[128]{0:T(128)S(1)} %multiply_multiply_fusion.1, f32[8192]{0:T(1024)S(1)} %bitcast.178, f32[128]{0:T(128)S(1)} %add_rsqrt_fusion.1, bf16[128,512]{1,0:T(8,128)(2,1)S(1)} %copy.97, ...), kind=kOutput, calls=%fused_computation.28 | convolution fusion | flops 2154299392 | bytes 21267456 | tf_op jit(solution)/shard_map/dot_general | solution.py:104
  202.9 1.9 collective-permute-start.2
  204.9 2.1 fusion.30
  207.0 2.2 fusion.32
  209.1 8.9 %fusion.109 = (bf16[128,1024]{1,0:T(8,128)(2,1)S(1)}, f32[128,1024]{1,0:T(8,128)}) fusion(bf16[128,8192]{1,0:T(8,128)(2,1)S(1)} %fusion.32, bf16[1,8192,1024]{2,1,0:T(8,128)(2,1)} %all-gather.9.cloned.1.call-done), kind=kOutput, calls=%fused_computation.131 | convolution fusion | flops 2147614720 | bytes 19660800 | tf_op jit(solution)/shard_map/dot_general | solution.py:89
  218.2 1.7 fusion.70
  219.9 3.3 %fusion.110 = (f32[4,8,128]{2,1,0:T(8,128)S(1)}, f32[4,8,128,128]{2,3,1,0:T(8,128)}) fusion(pred[128,128]{0,1:T(8,128)(4,1)S(1)} %copy-done.8, bf16[128,4,8,128]{0,3,2,1:T(8,128)(2,1)} %bitcast.171, bf16[128,4,128,1]{2,1,0,3:T(4,128)(2,1)S(1)} %bitcast.183), kind=kOutput, calls=%fused_computation.132 | convolution fusion | flops 136315008 | bytes 3309568 | tf_op jit(solution)/shard_map/sub | solution.py:44
  223.2 4.6 %fusion.57 = bf16[4,128,128]{2,1,0:T(8,128)(2,1)S(1)} fusion(bf16[128,4,8,128]{0,3,2,1:T(8,128)(2,1)} %bitcast.172, f32[4,128,128,8]{2,1,3,0:T(8,128)} %fusion.70, f32[4,8,128,128]{2,3,1,0:T(8,128)} %get-tuple-element.51, f32[4,8,128]{2,1,0:T(8,128)S(1)} %get-tuple-element.50), kind=kOutput, calls=%fused_computation.71 | convolution fusion | flops 137957504 | bytes 5390336 | tf_op jit(solution)/shard_map/hgqk,qhgd->khd/dot_general | solution.py:55
  228.0 2.0 fusion.55
  232.3 21.4 %collective-permute-done.2 = bf16[128,8192]{1,0:T(8,128)(2,1)} collective-permute-done((bf16[128,8192]{1,0:T(8,128)(2,1)}, bf16[128,8192]{1,0:T(8,128)(2,1)}, u32[]{:S(2)}, u32[]{:S(2)}) %collective-permute-start.2) | collective-permute-done | bytes 2097184 | tf_op jit(solution)/shard_map/ppermute | solution.py:19
  253.7 4.9 %all-to-all-start.1 = ((bf16[128,4,2048]{2,0,1:T(8,128)(2,1)}), bf16[128,4,2048]{2,0,1:T(8,128)(2,1)}, u32[]{:S(2)}, u32[]{:S(2)}) async-start(bf16[128,4,2048]{2,0,1:T(8,128)(2,1)} %bitcast.166), calls=%async_computation.1 | async-start | bytes 4194304 | tf_op jit(solution)/shard_map/all_to_all | solution.py:88
  258.8 13.6 %fusion.21 = bf16[128,8192]{1,0:T(8,128)(2,1)} fusion(bf16[128,1024]{1,0:T(8,128)(2,1)S(1)} %copy-done.3, bf16[1,8192,1024]{2,1,0:T(8,128)(2,1)} %all-gather.9.cloned.1.call-done, bf16[128,8192]{1,0:T(8,128)(2,1)} %collective-permute-done.1, f32[128]{0:T(128)S(1)} %multiply_multiply_fusion, f32[128]{0:T(128)S(1)} %add_rsqrt_fusion, f32[8192]{0:T(1024)S(1)} %bitcast.180), kind=kOutput, calls=%fused_computation.15 | convolution fusion | flops 2153775104 | bytes 21267456 | tf_op jit(solution)/shard_map/dot_general | solution.py:104
  272.4 1.9 collective-permute-start.4
  274.3 8.4 %all-to-all-done.1 = bf16[128,4,2048]{2,0,1:T(8,128)(2,1)} async-done(((bf16[128,4,2048]{2,0,1:T(8,128)(2,1)}), bf16[128,4,2048]{2,0,1:T(8,128)(2,1)}, u32[]{:S(2)}, u32[]{:S(2)}) %all-to-all-start.1) | async-done | bytes 2097184 | tf_op jit(solution)/shard_map/all_to_all | solution.py:88
  282.8 11.0 %fusion.24 = (f32[2048]{0:T(1024)S(1)}, bf16[1,2048,1024]{1,2,0:T(8,128)(2,1)}) fusion(bf16[1,2048,1024]{1,2,0:T(8,128)(2,1)} %copy.74, bf16[512,1024]{1,0:T(8,128)(2,1)} %all-gather.7.cloned.1.call-done, bf16[512,1024]{1,0:T(8,128)(2,1)} %all-gather.5.cloned.1.call-done, bf16[512,2048]{1,0:T(8,128)(2,1)} %bitcast.40, bf16[512,2048]{1,0:T(8,128)(2,1)} %bitcast.38), kind=kOutput, calls=%fused_computation.17 | convolution fusion | flops 4315936768 | bytes 14688256 | tf_op jit(solution)/shard_map/dot_general | solution.py:112
  293.7 6.4 %copy.75 = bf16[1,2048,1024]{2,1,0:T(8,128)(2,1)} copy(bf16[1,2048,1024]{1,2,0:T(8,128)(2,1)} %get-tuple-element.31) | data formatting | bytes 8388608
  300.1 5.2 %all_gather.15 = f32[8192]{0:T(1024)S(1)} all-gather(f32[2048]{0:T(1024)S(1)} %div.39), channel_id=1, replica_groups=mesh['pipe'=8,'dp'=4] {'dp'}, dimensions={0}, use_global_device_ids=true | all-gather | bytes 40960 | tf_op jit(solution)/shard_map/all_gather | solution.py:119
  305.8 1.9 bitcast_dynamic-update-slice_fusion.1
  307.6 15.4 %collective-permute-done.4 = bf16[128,8192]{1,0:T(8,128)(2,1)S(1)} collective-permute-done((bf16[128,8192]{1,0:T(8,128)(2,1)}, bf16[128,8192]{1,0:T(8,128)(2,1)S(1)}, u32[]{:S(2)}, u32[]{:S(2)}) %collective-permute-start.4) | collective-permute-done | bytes 2097184 | tf_op jit(solution)/shard_map/ppermute | solution.py:19
  (74 shorter events, 21.9 us)
Async XLA Ops:
  7.2 158.8 %all-gather.9.cloned.1.call-start = ((), (), s32[]{:S(2)}) async-start(), calls=%async_computation.4 | async-start | bytes 20971520 | tf_op jit(solution)/shard_map/all_gather | solution.py:72
  7.9 6.3 %copy-start.10 = (s32[1,1,2]{2,1,0:T(1,128)S(1)}, s32[1,1,2]{2,1,0:T(1,128)}, u32[]{:S(2)}) copy-start(s32[1,1,2]{2,1,0:T(1,128)} %param.8) | copy-start | bytes 28
  12.6 143.4 %collective-permute-start = (bf16[128,8192]{1,0:T(8,128)(2,1)}, bf16[128,8192]{1,0:T(8,128)(2,1)S(1)}, u32[]{:S(2)}, u32[]{:S(2)}) collective-permute-start(bf16[128,8192]{1,0:T(8,128)(2,1)} %get-tuple-element.33), channel_id=1, source_target_pairs={{0,28},{4,24},{8,20},{12,16},{16,12},{20,8},{24,4},{28,0},{1,29},{... | collective-permute-start | bytes 6291464 | tf_op jit(solution)/shard_map/ppermute | solution.py:24
  14.2 136.9 %collective-permute-start.3 = (s32[2]{0:T(128)S(1)}, s32[2]{0:T(128)S(1)}, u32[]{:S(2)}, u32[]{:S(2)}) collective-permute-start(s32[2]{0:T(128)S(1)} %bitcast.189), channel_id=1, source_target_pairs={{4,0},{8,4},{12,8},{16,12},{20,16},{24,20},{28,24},{5,1},{9,5},{13... | collective-permute-start | bytes 32 | tf_op jit(solution)/shard_map/ppermute | solution.py:19
  21.4 6.9 %copy-start.7 = (bf16[1,8192]{1,0:T(2,128)(2,1)S(1)}, bf16[1,8192]{1,0:T(2,128)(2,1)}, u32[]{:S(2)}) copy-start(bf16[1,8192]{1,0:T(2,128)(2,1)} %param.12) | copy-start | bytes 49156
  28.3 178.6 %copy-start.5 = (f32[1,8192]{1,0:T(1,128)}, f32[1,8192]{1,0:T(1,128)S(1)}, u32[]{:S(2)}) copy-start(f32[1,8192]{1,0:T(1,128)S(1)} %mul.192) | copy-start | bytes 98308
  37.2 4.0 %copy-start.9 = (s32[1,2,128]{2,1,0:T(2,128)S(1)}, s32[1,2,128]{2,1,0:T(2,128)}, u32[]{:S(2)}) copy-start(s32[1,2,128]{2,1,0:T(2,128)} %param.9) | copy-start | bytes 3076
  156.0 1.3 copy-start
  156.0 48.8 %collective-permute-start.1 = (bf16[128,8192]{1,0:T(8,128)(2,1)}, bf16[128,8192]{1,0:T(8,128)(2,1)}, u32[]{:S(2)}, u32[]{:S(2)}) collective-permute-start(bf16[128,8192]{1,0:T(8,128)(2,1)} %get-tuple-element.13), channel_id=1, source_target_pairs={{0,28},{4,24},{8,20},{12,16},{16,12},{20,8},{24,4},{28,0},{1,29},{... | collective-permute-start | bytes 6291464 | tf_op jit(solution)/shard_map/ppermute | solution.py:24
  161.0 92.7 %all-to-all-start = ((bf16[128,4,2048]{2,0,1:T(8,128)(2,1)}), bf16[128,4,2048]{2,0,1:T(8,128)(2,1)}, u32[]{:S(2)}, u32[]{:S(2)}) async-start(bf16[128,4,2048]{2,0,1:T(8,128)(2,1)} %bitcast.165), calls=%async_computation | async-start | bytes 4194304 | tf_op jit(solution)/shard_map/all_to_all | solution.py:88
  165.9 108.4 %all-gather.5.cloned.1.call-start = ((), (), s32[]{:S(2)}) async-start(), calls=%async_computation.2 | async-start | bytes 1310720 | tf_op jit(solution)/shard_map/all_gather | solution.py:99
  183.5 6.4 %copy-start.1 = (bf16[128,8192]{1,0:T(8,128)(2,1)S(1)}, bf16[128,8192]{1,0:T(8,128)(2,1)}, u32[]{:S(2)}) copy-start(bf16[128,8192]{1,0:T(8,128)(2,1)} %copy-done) | copy-start | bytes 6291460
  188.4 85.9 %all-gather.7.cloned.1.call-start = ((), (), s32[]{:S(2)}) async-start(), calls=%async_computation.3 | async-start | bytes 1310720 | tf_op jit(solution)/shard_map/all_gather | solution.py:99
  202.9 50.8 %collective-permute-start.2 = (bf16[128,8192]{1,0:T(8,128)(2,1)}, bf16[128,8192]{1,0:T(8,128)(2,1)}, u32[]{:S(2)}, u32[]{:S(2)}) collective-permute-start(bf16[128,8192]{1,0:T(8,128)(2,1)} %fusion.29), channel_id=1, source_target_pairs={{4,0},{8,4},{12,8},{16,12},{20,16},{24,20},{28,24},{5,1},{9,5},{13... | collective-permute-start | bytes 6291464 | tf_op jit(solution)/shard_map/ppermute | solution.py:19
  218.1 1.7 copy-start.8
  223.2 4.6 %copy-start.11 = (f32[4,8,128]{2,1,0:T(8,128)}, f32[4,8,128]{2,1,0:T(8,128)S(1)}, u32[]{:S(2)}) copy-start(f32[4,8,128]{2,1,0:T(8,128)S(1)} %get-tuple-element.50) | copy-start | bytes 49156
  253.7 4.9 %copy-start.3 = (bf16[128,1024]{1,0:T(8,128)(2,1)S(1)}, bf16[128,1024]{1,0:T(8,128)(2,1)}, u32[]{:S(2)}) copy-start(bf16[128,1024]{1,0:T(8,128)(2,1)} %pad_maximum_fusion.1) | copy-start | bytes 786436
  253.7 4.9 %copy-start.4 = (f32[128,1024]{1,0:T(8,128)S(1)}, f32[128,1024]{1,0:T(8,128)}, u32[]{:S(2)}) copy-start(f32[128,1024]{1,0:T(8,128)} %get-tuple-element.49) | copy-start | bytes 1572868
  253.7 5.1 %copy-start.6 = (f32[1,8192]{1,0:T(1,128)S(1)}, f32[1,8192]{1,0:T(1,128)}, u32[]{:S(2)}) copy-start(f32[1,8192]{1,0:T(1,128)} %copy-done.5) | copy-start | bytes 98308
  253.7 29.0 %all-to-all-start.1 = ((bf16[128,4,2048]{2,0,1:T(8,128)(2,1)}), bf16[128,4,2048]{2,0,1:T(8,128)(2,1)}, u32[]{:S(2)}, u32[]{:S(2)}) async-start(bf16[128,4,2048]{2,0,1:T(8,128)(2,1)} %bitcast.166), calls=%async_computation.1 | async-start | bytes 4194304 | tf_op jit(solution)/shard_map/all_to_all | solution.py:88
  272.4 50.7 %collective-permute-start.4 = (bf16[128,8192]{1,0:T(8,128)(2,1)}, bf16[128,8192]{1,0:T(8,128)(2,1)S(1)}, u32[]{:S(2)}, u32[]{:S(2)}) collective-permute-start(bf16[128,8192]{1,0:T(8,128)(2,1)} %fusion.21), channel_id=1, source_target_pairs={{4,0},{8,4},{12,8},{16,12},{20,16},{24,20},{28,24},{5,1},{9,5},{13... | collective-permute-start | bytes 6291464 | tf_op jit(solution)/shard_map/ppermute | solution.py:19
  323.3 2.0 copy-start.2
Sparse Core Ops, SparseCore 0:
  9.6 106.0 all-gather.8
  188.6 15.5 all-gather.4
  232.5 17.0 all-gather.6

commit v3 on v2

--- a/solution.py
+++ b/solution.py
@@ -85,7 +85,8 @@
         inputs_wide = arrived[slot].astype(jnp.float32)
         inverse = lax.rsqrt(jnp.mean(inputs_wide * inputs_wide, axis=-1, keepdims=True) + EPSILON)
         normed = (inputs_wide * inverse * gain_full).astype(jnp.bfloat16)
-        all_normed.append(lax.all_to_all(normed, "dp", split_axis=1, concat_axis=0, tiled=True))
+        sent, _ = lax.optimization_barrier((normed, full_weight))
+        all_normed.append(lax.all_to_all(sent, "dp", split_axis=1, concat_axis=0, tiled=True))
         projected = jnp.dot(normed, full_weight, preferred_element_type=jnp.float32)
         projected_low = projected.astype(jnp.bfloat16)
         head_span = projected_low.shape[-1] // 2

time: 333 us -> 329 us (0.988)
  waiting for transfers between devices: 155 us -> 146 us
  matrix products: 78.7 us -> 82.4 us
    ppermute x3, waiting for transfers between devices: 146 us -> 135 us  [shifted(): lax.ppermute(value, axis, [(source, source + steps) for source in range(l...]
    unnamed x31 -> x33, local copies, waits for them, and re-layouts: 23.6 us -> 23.9 us
  transfers between devices with their start and end apart: 10 -> 10, of which waited for: 4 -> 5; matrix products, arithmetic and copies ran while one was open for 39% -> 40% of each run, Pallas kernels for 0% -> 0%
where the time goes in v3:
time: 329 us; the launch traced here: 328 us
  waiting for transfers between devices  146 us (44%)
  matrix products  82.4 us (25%)
  local copies, waits for them, and re-layouts  40.6 us (12%)
  between operations  21.4 us (7%)
  starting transfers between devices  19.1 us (6%)
  other arithmetic  13.3 us (4%)
  blocking collectives  5.18 us (2%)
    ppermute x3, waiting for transfers between devices, shifted(): lax.ppermute(value, axis, [(source, source + steps) for source in range(l...  135 us
    dot_general x2, matrix products, local(): lax.dot_general(kv_grads, full_weight, (((1,), (1,)), ((), ())), preferre...  27.2 us
    unnamed x33, local copies, waits for them, and re-layouts  23.9 us
    dot_general x2, matrix products, local(): projected = jnp.dot(normed, full_weight, preferred_element_type=jnp.float32)  18.5 us
    dot_general x1, matrix products, local(): lax.dot_general(jnp.concatenate(all_normed), jnp.concatenate(all_grads),...  11 us
    all_to_all x2, starting transfers between devices, local(): lax.all_to_all(sent, 'dp', split_axis=1, concat_axis=0, tiled=True)  9.99 us
    dot_general x2, matrix products, attention_grads(): jnp.einsum('hgqk,qhgd->khd', score_grad, query_heads, preferred_element_t...  9.22 us
    all_to_all x2, waiting for transfers between devices, local(): lax.all_to_all(sent, 'dp', split_axis=1, concat_axis=0, tiled=True)  8.16 us
  transfers between devices with their start and end apart: 10, of which 5 were waited for; matrix products, arithmetic and copies ran while one was open for 40% of the time, Pallas kernels for 0%

profile of v3, /device:TPU:14, one launch (start us, length us, event | category | flops | bytes accessed | tf_op | source)
XLA Modules:
  0.0 328.2 jit_solution(13229384093093447860)
XLA Ops:
  8.0 4.7 %slice_bitcast_fusion = (bf16[128,8192]{1,0:T(8,128)(2,1)}, bf16[128,8192]{1,0:T(8,128)(2,1)}) fusion(bf16[1,2,128,8192]{3,2,1,0:T(8,128)(2,1)} %param.7), kind=kLoop, calls=%fused_computation.50 | loop fusion | bytes 8388608 | tf_op jit(solution)/shard_map/squeeze | solution.py:77
  14.2 3.4 %collective-permute-start.3 = (s32[2]{0:T(128)S(1)}, s32[2]{0:T(128)S(1)}, u32[]{:S(2)}, u32[]{:S(2)}) collective-permute-start(s32[2]{0:T(128)S(1)} %bitcast.179), channel_id=1, source_target_pairs={{4,0},{8,4},{12,8},{16,12},{20,16},{24,20},{28,24},{5,1},{9,5},{13... | collective-permute-start | bytes 32 | tf_op jit(solution)/shard_map/ppermute | solution.py:19
  21.4 6.9 %copy.74 = bf16[1,2048,1024]{1,2,0:T(8,128)(2,1)} copy(bf16[1,2048,1024]{2,1,0:T(8,128)(2,1)} %param.13) | data formatting | bytes 8388608 | tf_op args[6]
  29.6 4.0 %constant_dynamic-slice_fusion.2 = (bf16[1,1,128,4096]{3,2,1,0:T(8,128)(2,1)S(1)}, bf16[1,1,128,4096]{3,2,1,0:T(8,128)(2,1)}, bf16[1,1,128,4096]{3,2,1,0:T(8,128)(2,1)}, bf16[1,1,128,4096]{3,2,1,0:T(8,128)(2,1)}) fusion(bf16[1,2,128,4096]{3,2,1,0:T(8,128)(2,1)} %param.11, s32[]{:T(128)S(6)} %select_n.40, s32[]{:T(128)S(6)} %select_n.39, ...), kind=kLoop, calls=%fused_computation.95 | loop fusion | bytes 8388616 | tf_op jit(solution)/shard_map/jit(dynamic_index_in_dim)/dynamic_slice | solution.py:95
  33.6 2.3 copy.105
  38.9 2.3 copy.104
  41.9 109.2 %collective-permute-done.3 = s32[2]{0:T(128)S(1)} collective-permute-done((s32[2]{0:T(128)S(1)}, s32[2]{0:T(128)S(1)}, u32[]{:S(2)}, u32[]{:S(2)}) %collective-permute-start.3) | collective-permute-done | bytes 40 | tf_op jit(solution)/shard_map/ppermute | solution.py:19
  157.5 2.2 fusion.9
  159.7 8.9 %fusion.91 = (bf16[128,1024]{1,0:T(8,128)(2,1)S(1)}, f32[128,1024]{1,0:T(8,128)}) fusion(bf16[128,8192]{1,0:T(8,128)(2,1)S(1)} %fusion.9, bf16[1,8192,1024]{2,1,0:T(8,128)(2,1)} %all-gather.9.cloned.1.call-done), kind=kOutput, calls=%fused_computation.127 | convolution fusion | flops 2147614720 | bytes 19660800 | tf_op jit(solution)/shard_map/dot_general | solution.py:90
  169.4 3.0 fusion.54
  172.5 3.3 %fusion.92 = (f32[4,8,128]{2,1,0:T(8,128)S(1)}, f32[4,8,128,128]{2,3,1,0:T(8,128)}) fusion(pred[128,128]{0,1:T(8,128)(4,1)S(1)} %get-tuple-element.58, bf16[128,4,8,128]{0,3,2,1:T(8,128)(2,1)} %bitcast.163, bf16[128,4,128,1]{2,1,0,3:T(4,128)(2,1)S(1)} %bitcast.172), kind=kOutput, calls=%fused_computation.128 | convolution fusion | flops 136315008 | bytes 3309568 | tf_op jit(solution)/shard_map/sub | solution.py:44
  175.8 4.6 %fusion.36 = bf16[4,128,128]{2,1,0:T(8,128)(2,1)S(1)} fusion(bf16[128,4,8,128]{0,3,2,1:T(8,128)(2,1)} %bitcast.164, f32[4,128,128,8]{2,1,3,0:T(8,128)} %fusion.54, f32[4,8,128,128]{2,3,1,0:T(8,128)} %get-tuple-element.51, f32[4,8,128]{2,1,0:T(8,128)S(1)} %get-tuple-element.50), kind=kOutput, calls=%fused_computation.62 | convolution fusion | flops 137957504 | bytes 5390336 | tf_op jit(solution)/shard_map/hgqk,qhgd->khd/dot_general | solution.py:55
  180.6 3.0 fusion.34
  186.6 13.6 %fusion.11 = bf16[128,8192]{1,0:T(8,128)(2,1)} fusion(bf16[128,8192]{1,0:T(8,128)(2,1)} %copy-done.1, f32[128]{0:T(128)S(1)} %multiply_multiply_fusion.1, f32[8192]{0:T(1024)S(1)} %bitcast.168, f32[128]{0:T(128)S(1)} %add_rsqrt_fusion.1, bf16[1,8192,1024]{2,1,0:T(8,128)(2,1)} %all-gather.9.cloned.1.call-done, bf16[128,512]{1,0:T(8,128)(2,1)S(1)} %copy.97, ...), kind=kOutput, calls=%fused_computation.20 | convolution fusion | flops 2154299392 | bytes 21267456 | tf_op jit(solution)/shard_map/dot_general | solution.py:105
  200.2 1.9 collective-permute-start.2
  202.1 2.1 collective-permute-done.1
  204.2 2.1 fusion.12
  206.3 2.2 fusion.14
  210.5 4.9 %all-to-all-start.1 = ((bf16[128,4,2048]{2,0,1:T(8,128)(2,1)}), bf16[128,4,2048]{2,0,1:T(8,128)(2,1)}, u32[]{:S(2)}, u32[]{:S(2)}) async-start(bf16[128,4,2048]{2,0,1:T(8,128)(2,1)} %bitcast.155), calls=%async_computation.1 | async-start | bytes 4194304 | tf_op jit(solution)/shard_map/all_to_all | solution.py:89
  215.4 9.6 %fusion.95 = (bf16[128,1024]{1,0:T(8,128)(2,1)S(1)}, f32[128,1024]{1,0:T(8,128)}) fusion(bf16[128,8192]{1,0:T(8,128)(2,1)} %copy-done, bf16[1,8192,1024]{2,1,0:T(8,128)(2,1)} %all-gather.9.cloned.1.call-done), kind=kOutput, calls=%fused_computation.129 | convolution fusion | flops 2147614720 | bytes 19660800 | tf_op jit(solution)/shard_map/dot_general | solution.py:90
  226.8 3.3 %fusion.96 = (f32[4,8,128]{2,1,0:T(8,128)S(1)}, f32[4,8,128,128]{2,3,1,0:T(8,128)}) fusion(pred[128,128]{0,1:T(8,128)(4,1)S(1)} %copy-done.9, bf16[128,4,8,128]{0,3,2,1:T(8,128)(2,1)} %bitcast.161, bf16[128,4,128,1]{2,1,0,3:T(4,128)(2,1)S(1)} %bitcast.173), kind=kOutput, calls=%fused_computation.130 | convolution fusion | flops 136315008 | bytes 3309568 | tf_op jit(solution)/shard_map/sub | solution.py:44
  230.1 4.6 %fusion.37 = bf16[4,128,128]{2,1,0:T(8,128)(2,1)S(1)} fusion(bf16[128,4,8,128]{0,3,2,1:T(8,128)(2,1)} %bitcast.162, f32[4,128,128,8]{2,1,3,0:T(8,128)} %fusion.50, f32[4,8,128,128]{2,3,1,0:T(8,128)} %get-tuple-element.55, f32[4,8,128]{2,1,0:T(8,128)S(1)} %get-tuple-element.54), kind=kOutput, calls=%fused_computation.63 | convolution fusion | flops 137957504 | bytes 5390336 | tf_op jit(solution)/shard_map/hgqk,qhgd->khd/dot_general | solution.py:55
  234.9 2.0 fusion.35
  239.3 10.6 %collective-permute-done.2 = bf16[128,8192]{1,0:T(8,128)(2,1)} collective-permute-done((bf16[128,8192]{1,0:T(8,128)(2,1)}, bf16[128,8192]{1,0:T(8,128)(2,1)}, u32[]{:S(2)}, u32[]{:S(2)}) %collective-permute-start.2) | collective-permute-done | bytes 2097184 | tf_op jit(solution)/shard_map/ppermute | solution.py:19
  249.9 5.1 %all-to-all-start = ((bf16[128,4,2048]{2,0,1:T(8,128)(2,1)}), bf16[128,4,2048]{2,0,1:T(8,128)(2,1)}, u32[]{:S(2)}, u32[]{:S(2)}) async-start(bf16[128,4,2048]{2,0,1:T(8,128)(2,1)} %bitcast.156), calls=%async_computation | async-start | bytes 4194304 | tf_op jit(solution)/shard_map/all_to_all | solution.py:89
  255.1 13.6 %fusion.5 = bf16[128,8192]{1,0:T(8,128)(2,1)} fusion(bf16[128,1024]{1,0:T(8,128)(2,1)S(1)} %copy-done.3, bf16[128,8192]{1,0:T(8,128)(2,1)} %collective-permute-done.1, f32[128]{0:T(128)S(1)} %multiply_multiply_fusion, f32[128]{0:T(128)S(1)} %add_rsqrt_fusion, f32[8192]{0:T(1024)S(1)} %bitcast.170, bf16[1,8192,1024]{2,1,0:T(8,128)(2,1)} %all-gather.9.cloned.1.call-done), kind=kOutput, calls=%fused_computation.7 | convolution fusion | flops 2153775104 | bytes 21267456 | tf_op jit(solution)/shard_map/dot_general | solution.py:105
  268.7 2.2 collective-permute-start.4
  270.9 8.2 %all-to-all-done = bf16[128,4,2048]{2,0,1:T(8,128)(2,1)} async-done(((bf16[128,4,2048]{2,0,1:T(8,128)(2,1)}), bf16[128,4,2048]{2,0,1:T(8,128)(2,1)}, u32[]{:S(2)}, u32[]{:S(2)}) %all-to-all-start) | async-done | bytes 2097184 | tf_op jit(solution)/shard_map/all_to_all | solution.py:89
  279.1 11.0 %fusion.6 = (f32[2048]{0:T(1024)S(1)}, bf16[1,2048,1024]{1,2,0:T(8,128)(2,1)}) fusion(bf16[1,2048,1024]{1,2,0:T(8,128)(2,1)} %copy.74, bf16[512,1024]{1,0:T(8,128)(2,1)} %all-gather.7.cloned.1.call-done, bf16[512,1024]{1,0:T(8,128)(2,1)} %all-gather.5.cloned.1.call-done, bf16[512,2048]{1,0:T(8,128)(2,1)} %bitcast.40, bf16[512,2048]{1,0:T(8,128)(2,1)} %bitcast.38), kind=kOutput, calls=%fused_computation.9 | convolution fusion | flops 4315936768 | bytes 14688256 | tf_op jit(solution)/shard_map/dot_general | solution.py:113
  290.0 6.4 %copy.75 = bf16[1,2048,1024]{2,1,0:T(8,128)(2,1)} copy(bf16[1,2048,1024]{1,2,0:T(8,128)(2,1)} %get-tuple-element.35) | data formatting | bytes 8388608
  296.4 5.2 %all_gather.15 = f32[8192]{0:T(1024)S(1)} all-gather(f32[2048]{0:T(1024)S(1)} %div.39), channel_id=1, replica_groups=mesh['pipe'=8,'dp'=4] {'dp'}, dimensions={0}, use_global_device_ids=true | all-gather | bytes 40960 | tf_op jit(solution)/shard_map/all_gather | solution.py:120
  303.9 15.4 %collective-permute-done.4 = bf16[128,8192]{1,0:T(8,128)(2,1)S(1)} collective-permute-done((bf16[128,8192]{1,0:T(8,128)(2,1)}, bf16[128,8192]{1,0:T(8,128)(2,1)S(1)}, u32[]{:S(2)}, u32[]{:S(2)}) %collective-permute-start.4) | collective-permute-done | bytes 2097184 | tf_op jit(solution)/shard_map/ppermute | solution.py:19
  (76 shorter events, 25.1 us)
Async XLA Ops:
  7.2 152.6 %all-gather.9.cloned.1.call-start = ((), (), s32[]{:S(2)}) async-start(), calls=%async_computation.4 | async-start | bytes 20971520 | tf_op jit(solution)/shard_map/all_gather | solution.py:72
  7.9 6.3 %copy-start.11 = (s32[1,1,2]{2,1,0:T(1,128)S(1)}, s32[1,1,2]{2,1,0:T(1,128)}, u32[]{:S(2)}) copy-start(s32[1,1,2]{2,1,0:T(1,128)} %param.8) | copy-start | bytes 28
  7.9 263.0 %all-gather.5.cloned.1.call-start = ((), (), s32[]{:S(2)}) async-start(), calls=%async_computation.2 | async-start | bytes 1310720 | tf_op jit(solution)/shard_map/all_gather | solution.py:100
  12.7 143.6 %collective-permute-start = (bf16[128,8192]{1,0:T(8,128)(2,1)}, bf16[128,8192]{1,0:T(8,128)(2,1)S(1)}, u32[]{:S(2)}, u32[]{:S(2)}) collective-permute-start(bf16[128,8192]{1,0:T(8,128)(2,1)} %get-tuple-element.37), channel_id=1, source_target_pairs={{0,28},{4,24},{8,20},{12,16},{16,12},{20,8},{24,4},{28,0},{1,29},{... | collective-permute-start | bytes 6291464 | tf_op jit(solution)/shard_map/ppermute | solution.py:24
  14.2 136.9 %collective-permute-start.3 = (s32[2]{0:T(128)S(1)}, s32[2]{0:T(128)S(1)}, u32[]{:S(2)}, u32[]{:S(2)}) collective-permute-start(s32[2]{0:T(128)S(1)} %bitcast.179), channel_id=1, source_target_pairs={{4,0},{8,4},{12,8},{16,12},{20,16},{24,20},{28,24},{5,1},{9,5},{13... | collective-permute-start | bytes 32 | tf_op jit(solution)/shard_map/ppermute | solution.py:19
  21.4 6.9 %copy-start.8 = (bf16[1,8192]{1,0:T(2,128)(2,1)S(1)}, bf16[1,8192]{1,0:T(2,128)(2,1)}, u32[]{:S(2)}) copy-start(bf16[1,8192]{1,0:T(2,128)(2,1)} %param.12) | copy-start | bytes 49156
  28.3 178.0 %copy-start.5 = (f32[1,8192]{1,0:T(1,128)}, f32[1,8192]{1,0:T(1,128)S(1)}, u32[]{:S(2)}) copy-start(f32[1,8192]{1,0:T(1,128)S(1)} %mul.192) | copy-start | bytes 98308
  37.2 4.0 %copy-start.10 = (s32[1,2,128]{2,1,0:T(2,128)S(1)}, s32[1,2,128]{2,1,0:T(2,128)}, u32[]{:S(2)}) copy-start(s32[1,2,128]{2,1,0:T(2,128)} %param.9) | copy-start | bytes 3076
  156.3 1.3 copy-start.1
  156.3 48.0 %collective-permute-start.1 = (bf16[128,8192]{1,0:T(8,128)(2,1)}, bf16[128,8192]{1,0:T(8,128)(2,1)}, u32[]{:S(2)}, u32[]{:S(2)}) collective-permute-start(bf16[128,8192]{1,0:T(8,128)(2,1)} %get-tuple-element.15), channel_id=1, source_target_pairs={{0,28},{4,24},{8,20},{12,16},{16,12},{20,8},{24,4},{28,0},{1,29},{... | collective-permute-start | bytes 6291464 | tf_op jit(solution)/shard_map/ppermute | solution.py:24
  169.4 3.0 copy-start.7
  200.2 49.6 %collective-permute-start.2 = (bf16[128,8192]{1,0:T(8,128)(2,1)}, bf16[128,8192]{1,0:T(8,128)(2,1)}, u32[]{:S(2)}, u32[]{:S(2)}) collective-permute-start(bf16[128,8192]{1,0:T(8,128)(2,1)} %fusion.11), channel_id=1, source_target_pairs={{4,0},{8,4},{12,8},{16,12},{20,16},{24,20},{28,24},{5,1},{9,5},{13... | collective-permute-start | bytes 6291464 | tf_op jit(solution)/shard_map/ppermute | solution.py:19
  208.5 2.0 copy-start
  210.5 39.4 %all-to-all-start.1 = ((bf16[128,4,2048]{2,0,1:T(8,128)(2,1)}), bf16[128,4,2048]{2,0,1:T(8,128)(2,1)}, u32[]{:S(2)}, u32[]{:S(2)}) async-start(bf16[128,4,2048]{2,0,1:T(8,128)(2,1)} %bitcast.155), calls=%async_computation.1 | async-start | bytes 4194304 | tf_op jit(solution)/shard_map/all_to_all | solution.py:89
  215.4 55.5 %all-gather.7.cloned.1.call-start = ((), (), s32[]{:S(2)}) async-start(), calls=%async_computation.3 | async-start | bytes 1310720 | tf_op jit(solution)/shard_map/all_gather | solution.py:100
  225.1 1.7 copy-start.9
  230.1 4.6 %copy-start.12 = (f32[4,8,128]{2,1,0:T(8,128)}, f32[4,8,128]{2,1,0:T(8,128)S(1)}, u32[]{:S(2)}) copy-start(f32[4,8,128]{2,1,0:T(8,128)S(1)} %get-tuple-element.54) | copy-start | bytes 49156
  249.9 5.1 %copy-start.3 = (bf16[128,1024]{1,0:T(8,128)(2,1)S(1)}, bf16[128,1024]{1,0:T(8,128)(2,1)}, u32[]{:S(2)}) copy-start(bf16[128,1024]{1,0:T(8,128)(2,1)} %pad_maximum_fusion.1) | copy-start | bytes 786436
  249.9 5.1 %copy-start.4 = (f32[128,1024]{1,0:T(8,128)S(1)}, f32[128,1024]{1,0:T(8,128)}, u32[]{:S(2)}) copy-start(f32[128,1024]{1,0:T(8,128)} %get-tuple-element.53) | copy-start | bytes 1572868
  249.9 5.2 %copy-start.6 = (f32[1,8192]{1,0:T(1,128)S(1)}, f32[1,8192]{1,0:T(1,128)}, u32[]{:S(2)}) copy-start(f32[1,8192]{1,0:T(1,128)} %copy-done.5) | copy-start | bytes 98308
  249.9 29.2 %all-to-all-start = ((bf16[128,4,2048]{2,0,1:T(8,128)(2,1)}), bf16[128,4,2048]{2,0,1:T(8,128)(2,1)}, u32[]{:S(2)}, u32[]{:S(2)}) async-start(bf16[128,4,2048]{2,0,1:T(8,128)(2,1)} %bitcast.156), calls=%async_computation | async-start | bytes 4194304 | tf_op jit(solution)/shard_map/all_to_all | solution.py:89
  268.7 50.7 %collective-permute-start.4 = (bf16[128,8192]{1,0:T(8,128)(2,1)}, bf16[128,8192]{1,0:T(8,128)(2,1)S(1)}, u32[]{:S(2)}, u32[]{:S(2)}) collective-permute-start(bf16[128,8192]{1,0:T(8,128)(2,1)} %fusion.5), channel_id=1, source_target_pairs={{4,0},{8,4},{12,8},{16,12},{20,16},{24,20},{28,24},{5,1},{9,5},{13... | collective-permute-start | bytes 6291464 | tf_op jit(solution)/shard_map/ppermute | solution.py:19
  319.6 2.0 copy-start.2
Sparse Core Ops, SparseCore 0:
  9.6 106.0 all-gather.8
  185.5 15.6 all-gather.4
  239.4 15.1 all-gather.6

commit v4 on v3

--- a/solution.py
+++ b/solution.py
@@ -79,7 +79,7 @@
             arrived[-1], block = lax.optimization_barrier((arrived[-1], block))
         arrived.append(mirrored(block, "pipe"))
 
-    all_normed, all_grads, shifts = [], [], []
+    all_normed, all_grads, shifts, places = [], [], [], []
     for slot in range(micro_count):
         micro = jnp.argmax(order == slot)
         inputs_wide = arrived[slot].astype(jnp.float32)
@@ -98,15 +98,27 @@
             lax.dynamic_index_in_dim(segment_ids[0], micro, keepdims=False),
         )
         all_grads.append(lax.all_gather(kv_grads, "dp", axis=0, tiled=True))
-        if shifts:
-            kv_grads, shifts[-1] = lax.optimization_barrier((kv_grads, shifts[-1]))
         inner = jnp.sum(kv_grads.astype(jnp.float32) * projected, axis=-1, keepdims=True)
         inner = inner * (inverse * inverse / feature_count)
-        normed_grad = lax.dot_general(
-            kv_grads, full_weight, (((1,), (1,)), ((), ())), preferred_element_type=jnp.float32
-        )
-        input_grad = (inverse * gain_full * normed_grad - inputs_wide * inner).astype(jnp.bfloat16)
-        shifts.append(shifted(input_grad, "pipe", -1))
+        pieces = 1 if slot + 1 < micro_count else 2
+        width = feature_count // pieces
+        for piece in range(pieces):
+            if piece and len(shifts) > piece:
+                kv_grads, shifts[0], all_normed[-1] = lax.optimization_barrier(
+                    (kv_grads, shifts[0], all_normed[-1])
+                )
+            span = slice(piece * width, (piece + 1) * width)
+            normed_grad = lax.dot_general(
+                kv_grads,
+                full_weight[span],
+                (((1,), (1,)), ((), ())),
+                preferred_element_type=jnp.float32,
+            )
+            input_grad = (
+                inverse * gain_full[span] * normed_grad - inputs_wide[:, span] * inner
+            ).astype(jnp.bfloat16)
+            shifts.append(shifted(input_grad, "pipe", -1))
+            places.append((slot, piece * width))
         if slot + 1 < micro_count:
             arrived[slot + 1], _ = lax.optimization_barrier((arrived[slot + 1], input_grad))
 
@@ -119,9 +131,9 @@
     gain_part = jnp.sum(weight_wide * local_weight.astype(jnp.float32), axis=-1) / gain_local
     gain_grad = lax.all_gather(gain_part, "dp", axis=0, tiled=True)
     upstream = jnp.zeros((micro_count, seq_len, feature_count), jnp.bfloat16)
-    for slot in range(micro_count):
-        upstream = lax.dynamic_update_index_in_dim(
-            upstream, shifts[slot], jnp.argmax(order_next == slot), 0
+    for moved, (slot, column) in zip(shifts, places):
+        upstream = lax.dynamic_update_slice(
+            upstream, moved[None], (jnp.argmax(order_next == slot), 0, column)
         )
     return (upstream[None], weight_wide.astype(jnp.bfloat16)[None], gain_grad[None])
 

time: 329 us -> 331 us (level)
  waiting for transfers between devices: 146 us -> 128 us
  local copies, waits for them, and re-layouts: 40.6 us -> 49.1 us
  other arithmetic: 13.3 us -> 17.5 us
    ppermute x3 -> x4, waiting for transfers between devices: 135 us -> 108 us  [shifted(): lax.ppermute(value, axis, [(source, source + steps) for source in range(l...]
    all_to_all x2, waiting for transfers between devices: 8.16 us -> 17.2 us  [local(): lax.all_to_all(sent, 'dp', split_axis=1, concat_axis=0, tiled=True)]
    dynamic_update_slice x2 -> x3, local copies, waits for them, and re-layouts: 2.1 us -> 6.42 us  [local(): lax.dynamic_update_slice(upstream, moved[None], (jnp.argmax(order_next ==...]
    convert_element_type x0 -> x1, other arithmetic: none -> 4.04 us  [local(): inputs_wide = arrived[slot].astype(jnp.float32)]
    ppermute x3 -> x4, starting transfers between devices: 7.47 us -> 9.6 us  [shifted(): lax.ppermute(value, axis, [(source, source + steps) for source in range(l...]
    dot_general x2 -> x3, matrix products: 27.2 us -> 28.8 us  [local(): lax.dot_general(kv_grads, full_weight[span], (((1,), (1,)), ((), ())), pr...]
    unnamed x33 -> x31, local copies, waits for them, and re-layouts: 23.9 us -> 23.3 us
  transfers between devices with their start and end apart: 10 -> 11, of which waited for: 5 -> 4; matrix products, arithmetic and copies ran while one was open for 40% -> 45% of each run, Pallas kernels for 0% -> 0%
where the time goes in v4:
time: 331 us; the launch traced here: 328 us
  waiting for transfers between devices  128 us (39%)
  matrix products  84.7 us (26%)
  local copies, waits for them, and re-layouts  49.1 us (15%)
  between operations  21.7 us (7%)
  starting transfers between devices  21.6 us (7%)
  other arithmetic  17.5 us (5%)
  blocking collectives  5.18 us (2%)
    ppermute x4, waiting for transfers between devices, shifted(): lax.ppermute(value, axis, [(source, source + steps) for source in range(l...  108 us
    dot_general x3, matrix products, local(): lax.dot_general(kv_grads, full_weight[span], (((1,), (1,)), ((), ())), pr...  28.8 us
    unnamed x31, local copies, waits for them, and re-layouts  23.3 us
    dot_general x2, matrix products, local(): projected = jnp.dot(normed, full_weight, preferred_element_type=jnp.float32)  19.1 us
    all_to_all x2, waiting for transfers between devices, local(): lax.all_to_all(sent, 'dp', split_axis=1, concat_axis=0, tiled=True)  17.2 us
    all_to_all x2, starting transfers between devices, local(): lax.all_to_all(sent, 'dp', split_axis=1, concat_axis=0, tiled=True)  10.3 us
    dot_general x1, matrix products, local(): lax.dot_general(jnp.concatenate(all_normed), jnp.concatenate(all_grads),...  10.3 us
    ppermute x4, starting transfers between devices, shifted(): lax.ppermute(value, axis, [(source, source + steps) for source in range(l...  9.6 us
  transfers between devices with their start and end apart: 11, of which 4 were waited for; matrix products, arithmetic and copies ran while one was open for 45% of the time, Pallas kernels for 0%

profile of v4, /device:TPU:14, one launch (start us, length us, event | category | flops | bytes accessed | tf_op | source)
XLA Modules:
  0.0 327.7 jit_solution(10782678166748104599)
XLA Ops:
  8.0 4.7 %slice_bitcast_fusion.16 = (bf16[128,8192]{1,0:T(8,128)(2,1)}, bf16[128,8192]{1,0:T(8,128)(2,1)}) fusion(bf16[1,2,128,8192]{3,2,1,0:T(8,128)(2,1)} %param.7), kind=kLoop, calls=%fused_computation.54 | loop fusion | bytes 8388608 | tf_op jit(solution)/shard_map/squeeze | solution.py:77
  14.2 3.4 %collective-permute-start.3 = (s32[2]{0:T(128)S(1)}, s32[2]{0:T(128)S(1)}, u32[]{:S(2)}, u32[]{:S(2)}) collective-permute-start(s32[2]{0:T(128)S(1)} %bitcast.200), channel_id=1, source_target_pairs={{4,0},{8,4},{12,8},{16,12},{20,16},{24,20},{28,24},{5,1},{9,5},{13... | collective-permute-start | bytes 32 | tf_op jit(solution)/shard_map/ppermute | solution.py:19
  22.7 4.8 %constant_dynamic-slice_fusion.2 = (bf16[1,1,128,4096]{3,2,1,0:T(8,128)(2,1)S(1)}, bf16[1,1,128,4096]{3,2,1,0:T(8,128)(2,1)}, bf16[1,1,128,4096]{3,2,1,0:T(8,128)(2,1)}, bf16[1,1,128,4096]{3,2,1,0:T(8,128)(2,1)}) fusion(bf16[1,2,128,4096]{3,2,1,0:T(8,128)(2,1)} %param.11, s32[]{:T(128)S(6)} %select_n.40, s32[]{:T(128)S(6)} %select_n.39, ...), kind=kLoop, calls=%fused_computation.101 | loop fusion | bytes 8388616 | tf_op jit(solution)/shard_map/jit(dynamic_index_in_dim)/dynamic_slice | solution.py:95
  27.5 6.6 %copy.74 = bf16[1,2048,1024]{1,2,0:T(8,128)(2,1)} copy(bf16[1,2048,1024]{2,1,0:T(8,128)(2,1)} %param.13) | data formatting | bytes 8388608 | tf_op args[6]
  34.2 2.3 copy.105
  39.4 2.3 copy.104
  43.1 107.9 %collective-permute-done.3 = s32[2]{0:T(128)S(1)} collective-permute-done((s32[2]{0:T(128)S(1)}, s32[2]{0:T(128)S(1)}, u32[]{:S(2)}, u32[]{:S(2)}) %collective-permute-start.3) | collective-permute-done | bytes 40 | tf_op jit(solution)/shard_map/ppermute | solution.py:19
  160.2 8.9 %fusion.94 = (bf16[128,1024]{1,0:T(8,128)(2,1)S(1)}, f32[128,1024]{1,0:T(8,128)}) fusion(bf16[128,8192]{1,0:T(8,128)(2,1)S(1)} %fusion.15, bf16[1,8192,1024]{2,1,0:T(8,128)(2,1)} %all-gather.9.cloned.1.call-done), kind=kOutput, calls=%fused_computation.133 | convolution fusion | flops 2147614720 | bytes 19660800 | tf_op jit(solution)/shard_map/dot_general | solution.py:90
  169.8 3.1 fusion.57
  172.9 3.3 %fusion.95 = (f32[4,8,128]{2,1,0:T(8,128)S(1)}, f32[4,8,128,128]{2,3,1,0:T(8,128)}) fusion(pred[128,128]{0,1:T(8,128)(4,1)S(1)} %get-tuple-element.62, bf16[128,4,8,128]{0,3,2,1:T(8,128)(2,1)} %bitcast.183, bf16[128,4,128,1]{2,1,0,3:T(4,128)(2,1)S(1)} %bitcast.191), kind=kOutput, calls=%fused_computation.134 | convolution fusion | flops 136315008 | bytes 3309568 | tf_op jit(solution)/shard_map/sub | solution.py:44
  176.2 4.8 %fusion.39 = bf16[4,128,128]{2,1,0:T(8,128)(2,1)S(1)} fusion(bf16[128,4,8,128]{0,3,2,1:T(8,128)(2,1)} %bitcast.184, f32[4,128,128,8]{2,1,3,0:T(8,128)} %fusion.57, f32[4,8,128,128]{2,3,1,0:T(8,128)} %get-tuple-element.55, f32[4,8,128]{2,1,0:T(8,128)S(1)} %get-tuple-element.54), kind=kOutput, calls=%fused_computation.66 | convolution fusion | flops 137957504 | bytes 5390336 | tf_op jit(solution)/shard_map/hgqk,qhgd->khd/dot_general | solution.py:55
  181.2 3.0 fusion.37
  186.4 13.5 %fusion.17 = bf16[128,8192]{1,0:T(8,128)(2,1)} fusion(bf16[128,8192]{1,0:T(8,128)(2,1)} %copy-done.1, f32[128]{0:T(128)S(1)} %multiply_multiply_fusion.1, f32[8192]{0:T(1024)S(1)} %bitcast.188, f32[128]{0:T(128)S(1)} %add_rsqrt_fusion.1, bf16[1,8192,1024]{2,1,0:T(8,128)(2,1)} %all-gather.9.cloned.1.call-done, bf16[128,512]{1,0:T(8,128)(2,1)S(1)} %copy.97, ...), kind=kOutput, calls=%fused_computation.24 | convolution fusion | flops 2154299392 | bytes 21267456 | tf_op jit(solution)/shard_map/dot_general | solution.py:111
  206.7 4.0 %convert_element_type.91 = f32[128,8192]{1,0:T(8,128)} convert(bf16[128,8192]{1,0:T(8,128)(2,1)} %collective-permute-done.1) | non-fusion elementwise | flops 1048576 | bytes 6291456 | tf_op jit(solution)/shard_map/convert_element_type | solution.py:85
  210.8 2.2 multiply_convert_fusion
  212.9 10.2 %fusion.98 = (bf16[128,1024]{1,0:T(8,128)(2,1)S(1)}, f32[128,1024]{1,0:T(8,128)}) fusion(bf16[128,8192]{1,0:T(8,128)(2,1)S(1)} %multiply_convert_fusion, bf16[1,8192,1024]{2,1,0:T(8,128)(2,1)} %all-gather.9.cloned.1.call-done), kind=kOutput, calls=%fused_computation.135 | convolution fusion | flops 2147614720 | bytes 19660800 | tf_op jit(solution)/shard_map/dot_general | solution.py:90
  223.3 4.0 %fusion.99 = (f32[4,8,128]{2,1,0:T(8,128)}, f32[4,8,128,128]{2,3,1,0:T(8,128)}) fusion(pred[128,128]{0,1:T(8,128)(4,1)} %get-tuple-element.63, bf16[128,4,8,128]{0,3,2,1:T(8,128)(2,1)} %bitcast.181, bf16[128,4,128,1]{2,1,0,3:T(4,128)(2,1)S(1)} %bitcast.192), kind=kOutput, calls=%fused_computation.136 | convolution fusion | flops 136315008 | bytes 3309568 | tf_op jit(solution)/shard_map/sub | solution.py:44
  229.0 4.6 %fusion.40 = bf16[4,128,128]{2,1,0:T(8,128)(2,1)S(1)} fusion(bf16[128,4,8,128]{0,3,2,1:T(8,128)(2,1)} %bitcast.182, f32[4,128,128,8]{2,1,3,0:T(8,128)} %fusion.53, f32[4,8,128,128]{2,3,1,0:T(8,128)} %get-tuple-element.59, f32[4,8,128]{2,1,0:T(8,128)S(1)} %copy-done.11), kind=kOutput, calls=%fused_computation.67 | convolution fusion | flops 137957504 | bytes 5390336 | tf_op jit(solution)/shard_map/hgqk,qhgd->khd/dot_general | solution.py:55
  233.7 3.1 copy.137
  236.8 4.9 %all-to-all-start = ((bf16[128,4,2048]{2,0,1:T(8,128)(2,1)}), bf16[128,4,2048]{2,0,1:T(8,128)(2,1)}, u32[]{:S(2)}, u32[]{:S(2)}) async-start(bf16[128,4,2048]{2,0,1:T(8,128)(2,1)} %bitcast.175), calls=%async_computation | async-start | bytes 4194304 | tf_op jit(solution)/shard_map/all_to_all | solution.py:89
  247.0 7.4 %fusion.12 = bf16[128,4096]{1,0:T(8,128)(2,1)} fusion(bf16[1,8192,1024]{2,1,0:T(8,128)(2,1)} %all-gather.9.cloned.1.call-done, f32[128,8192]{1,0:T(8,128)S(1)} %copy-done.2, f32[128]{0:T(128)S(1)} %multiply_multiply_fusion, f32[4096]{0:T(1024)S(1)} %bitcast.199, f32[128]{0:T(128)S(1)} %add_rsqrt_fusion, bf16[128,512]{1,0:T(8,128)(2,1)S(1)} %copy.103, ...), kind=kOutput, calls=%fused_computation.19 | convolution fusion | flops 1076887552 | bytes 11813888 | tf_op jit(solution)/shard_map/dot_general | solution.py:111
  257.0 8.9 %all-to-all-done = bf16[128,4,2048]{2,0,1:T(8,128)(2,1)} async-done(((bf16[128,4,2048]{2,0,1:T(8,128)(2,1)}), bf16[128,4,2048]{2,0,1:T(8,128)(2,1)}, u32[]{:S(2)}, u32[]{:S(2)}) %all-to-all-start) | async-done | bytes 2097184 | tf_op jit(solution)/shard_map/all_to_all | solution.py:89
  265.9 5.4 %all-to-all-start.1 = ((bf16[128,4,2048]{2,0,1:T(8,128)(2,1)}), bf16[128,4,2048]{2,0,1:T(8,128)(2,1)S(1)}, u32[]{:S(2)}, u32[]{:S(2)}) async-start(bf16[128,4,2048]{2,0,1:T(8,128)(2,1)} %bitcast.171), calls=%async_computation.1 | async-start | bytes 4194304 | tf_op jit(solution)/shard_map/all_to_all | solution.py:89
  271.3 7.9 %fusion.11 = bf16[128,4096]{1,0:T(8,128)(2,1)} fusion(bf16[128,1024]{1,0:T(8,128)(2,1)S(1)} %copy-done.4, bf16[1,8192,1024]{2,1,0:T(8,128)(2,1)} %all-gather.9.cloned.1.call-done, f32[128,8192]{1,0:T(8,128)} %convert_element_type.91, f32[4096]{0:T(1024)S(1)} %bitcast.198, f32[128]{0:T(128)S(1)} %multiply_multiply_fusion, f32[128]{0:T(128)S(1)} %add_rsqrt_fusion), kind=kOutput, calls=%fused_computation.18 | convolution fusion | flops 1076363264 | bytes 11813888 | tf_op jit(solution)/shard_map/dot_general | solution.py:111
  279.3 2.2 collective-permute-start.5
  281.4 2.5 broadcast_in_dim.30
  283.9 3.1 bitcast_dynamic-update-slice_fusion
  287.0 8.3 %all-to-all-done.1 = bf16[128,4,2048]{2,0,1:T(8,128)(2,1)S(1)} async-done(((bf16[128,4,2048]{2,0,1:T(8,128)(2,1)}), bf16[128,4,2048]{2,0,1:T(8,128)(2,1)S(1)}, u32[]{:S(2)}, u32[]{:S(2)}) %all-to-all-start.1) | async-done | bytes 2097184 | tf_op jit(solution)/shard_map/all_to_all | solution.py:89
  295.3 10.3 %fusion.6 = (f32[2048]{0:T(1024)S(1)}, bf16[1,2048,1024]{1,2,0:T(8,128)(2,1)}) fusion(bf16[1,2048,1024]{1,2,0:T(8,128)(2,1)} %copy.74, bf16[512,1024]{1,0:T(8,128)(2,1)} %all-gather.7.cloned.1.call-done, bf16[512,1024]{1,0:T(8,128)(2,1)} %all-gather.5.cloned.1.call-done, bf16[512,2048]{1,0:T(8,128)(2,1)} %bitcast.36, bf16[512,2048]{1,0:T(8,128)(2,1)S(1)} %bitcast.180), kind=kOutput, calls=%fused_computation.10 | convolution fusion | flops 4315936768 | bytes 14688256 | tf_op jit(solution)/shard_map/dot_general | solution.py:125
  305.6 6.4 %copy.75 = bf16[1,2048,1024]{2,1,0:T(8,128)(2,1)} copy(bf16[1,2048,1024]{1,2,0:T(8,128)(2,1)} %get-tuple-element.37) | data formatting | bytes 8388608
  312.0 5.2 %all_gather.15 = f32[8192]{0:T(1024)S(1)} all-gather(f32[2048]{0:T(1024)S(1)} %div.39), channel_id=1, replica_groups=mesh['pipe'=8,'dp'=4] {'dp'}, dimensions={0}, use_global_device_ids=true | all-gather | bytes 40960 | tf_op jit(solution)/shard_map/all_gather | solution.py:132
  317.2 2.3 bitcast_dynamic-update-slice_fusion.2
  (80 shorter events, 34.4 us)
Async XLA Ops:
  7.2 153.0 %all-gather.9.cloned.1.call-start = ((), (), s32[]{:S(2)}) async-start(), calls=%async_computation.4 | async-start | bytes 20971520 | tf_op jit(solution)/shard_map/all_gather | solution.py:72
  7.9 6.3 %copy-start.10 = (s32[1,1,2]{2,1,0:T(1,128)S(1)}, s32[1,1,2]{2,1,0:T(1,128)}, u32[]{:S(2)}) copy-start(s32[1,1,2]{2,1,0:T(1,128)} %param.8) | copy-start | bytes 28
  7.9 279.1 %all-gather.5.cloned.1.call-start = ((), (), s32[]{:S(2)}) async-start(), calls=%async_computation.2 | async-start | bytes 1310720 | tf_op jit(solution)/shard_map/all_gather | solution.py:100
  12.6 144.0 %collective-permute-start = (bf16[128,8192]{1,0:T(8,128)(2,1)}, bf16[128,8192]{1,0:T(8,128)(2,1)S(1)}, u32[]{:S(2)}, u32[]{:S(2)}) collective-permute-start(bf16[128,8192]{1,0:T(8,128)(2,1)} %get-tuple-element.39), channel_id=1, source_target_pairs={{0,28},{4,24},{8,20},{12,16},{16,12},{20,8},{24,4},{28,0},{1,29},{... | collective-permute-start | bytes 6291464 | tf_op jit(solution)/shard_map/ppermute | solution.py:24
  14.2 136.9 %collective-permute-start.3 = (s32[2]{0:T(128)S(1)}, s32[2]{0:T(128)S(1)}, u32[]{:S(2)}, u32[]{:S(2)}) collective-permute-start(s32[2]{0:T(128)S(1)} %bitcast.200), channel_id=1, source_target_pairs={{4,0},{8,4},{12,8},{16,12},{20,16},{24,20},{28,24},{5,1},{9,5},{13... | collective-permute-start | bytes 32 | tf_op jit(solution)/shard_map/ppermute | solution.py:19
  27.5 6.6 %copy-start.6 = (bf16[1,8192]{1,0:T(2,128)(2,1)S(1)}, bf16[1,8192]{1,0:T(2,128)(2,1)}, u32[]{:S(2)}) copy-start(bf16[1,8192]{1,0:T(2,128)(2,1)} %param.12) | copy-start | bytes 49156
  37.8 4.0 %copy-start.9 = (s32[1,2,128]{2,1,0:T(2,128)S(1)}, s32[1,2,128]{2,1,0:T(2,128)}, u32[]{:S(2)}) copy-start(s32[1,2,128]{2,1,0:T(2,128)} %param.9) | copy-start | bytes 3076
  156.6 1.3 copy-start.1
  156.7 48.0 %collective-permute-start.1 = (bf16[128,8192]{1,0:T(8,128)(2,1)}, bf16[128,8192]{1,0:T(8,128)(2,1)}, u32[]{:S(2)}, u32[]{:S(2)}) collective-permute-start(bf16[128,8192]{1,0:T(8,128)(2,1)} %get-tuple-element.16), channel_id=1, source_target_pairs={{0,28},{4,24},{8,20},{12,16},{16,12},{20,8},{24,4},{28,0},{1,29},{... | collective-permute-start | bytes 6291464 | tf_op jit(solution)/shard_map/ppermute | solution.py:24
  169.8 3.1 copy-start.5
  199.9 71.4 %collective-permute-start.2 = (bf16[128,8192]{1,0:T(8,128)(2,1)}, bf16[128,8192]{1,0:T(8,128)(2,1)}, u32[]{:S(2)}, u32[]{:S(2)}) collective-permute-start(bf16[128,8192]{1,0:T(8,128)(2,1)} %fusion.17), channel_id=1, source_target_pairs={{4,0},{8,4},{12,8},{16,12},{20,16},{24,20},{28,24},{5,1},{9,5},{13... | collective-permute-start | bytes 6291464 | tf_op jit(solution)/shard_map/ppermute | solution.py:19
  212.9 10.2 %copy-start = (bf16[128,8192]{1,0:T(8,128)(2,1)}, bf16[128,8192]{1,0:T(8,128)(2,1)S(1)}, u32[]{:S(2)}) copy-start(bf16[128,8192]{1,0:T(8,128)(2,1)S(1)} %multiply_convert_fusion) | copy-start | bytes 6291460
  227.3 1.7 copy-start.11
  236.8 29.1 %all-to-all-start = ((bf16[128,4,2048]{2,0,1:T(8,128)(2,1)}), bf16[128,4,2048]{2,0,1:T(8,128)(2,1)}, u32[]{:S(2)}, u32[]{:S(2)}) async-start(bf16[128,4,2048]{2,0,1:T(8,128)(2,1)} %bitcast.175), calls=%async_computation | async-start | bytes 4194304 | tf_op jit(solution)/shard_map/all_to_all | solution.py:89
  241.8 45.2 %all-gather.7.cloned.1.call-start = ((), (), s32[]{:S(2)}) async-start(), calls=%async_computation.3 | async-start | bytes 1310720 | tf_op jit(solution)/shard_map/all_gather | solution.py:100
  243.8 1.7 copy-start.3
  244.0 3.0 copy-start.2
  244.0 3.0 copy-start.8
  254.3 62.8 %collective-permute-start.4 = (bf16[128,4096]{1,0:T(8,128)(2,1)}, bf16[128,4096]{1,0:T(8,128)(2,1)}, u32[]{:S(2)}, u32[]{:S(2)}) collective-permute-start(bf16[128,4096]{1,0:T(8,128)(2,1)} %fusion.12), channel_id=1, source_target_pairs={{4,0},{8,4},{12,8},{16,12},{20,16},{24,20},{28,24},{5,1},{9,5},{13... | collective-permute-start | bytes 3145736 | tf_op jit(solution)/shard_map/ppermute | solution.py:19
  265.9 5.4 %copy-start.4 = (bf16[128,1024]{1,0:T(8,128)(2,1)S(1)}, bf16[128,1024]{1,0:T(8,128)(2,1)}, u32[]{:S(2)}) copy-start(bf16[128,1024]{1,0:T(8,128)(2,1)} %pad_maximum_fusion.1) | copy-start | bytes 786436
  265.9 5.4 %copy-start.7 = (f32[1,4096]{1,0:T(1,128)S(1)}, f32[1,4096]{1,0:T(1,128)}, u32[]{:S(2)}) copy-start(f32[1,4096]{1,0:T(1,128)} %get-tuple-element.48) | copy-start | bytes 49156
  265.9 29.4 %all-to-all-start.1 = ((bf16[128,4,2048]{2,0,1:T(8,128)(2,1)}), bf16[128,4,2048]{2,0,1:T(8,128)(2,1)S(1)}, u32[]{:S(2)}, u32[]{:S(2)}) async-start(bf16[128,4,2048]{2,0,1:T(8,128)(2,1)} %bitcast.171), calls=%async_computation.1 | async-start | bytes 4194304 | tf_op jit(solution)/shard_map/all_to_all | solution.py:89
  279.3 40.2 %collective-permute-start.5 = (bf16[128,4096]{1,0:T(8,128)(2,1)}, bf16[128,4096]{1,0:T(8,128)(2,1)S(1)}, u32[]{:S(2)}, u32[]{:S(2)}) collective-permute-start(bf16[128,4096]{1,0:T(8,128)(2,1)} %fusion.11), channel_id=1, source_target_pairs={{4,0},{8,4},{12,8},{16,12},{20,16},{24,20},{28,24},{5,1},{9,5},{13... | collective-permute-start | bytes 3145736 | tf_op jit(solution)/shard_map/ppermute | solution.py:19
Sparse Core Ops, SparseCore 0:
  9.6 106.0 all-gather.8
  210.9 15.1 all-gather.4
  257.1 16.5 all-gather.6
